TPU v7x, 32 devices: a whole 2x2x4 slice. The times are simulated.
32 devices in a mesh: row: 4 (over y, x), col: 8 (over z, core).
Axes of the slice: x: 2, y: 2, z: 4, core: 2. Of those that a mesh axis runs over, the one named last changes fastest.
Arguments:
- amps: float32 [4096, 9216], P('row', 'col'), may hold values from -6 to 6
- ladder_ints: float32 [4096, 4096], P('row', 'col'), may hold values from -0.25 to 0.25
- cycle_ints: float32 [6144, 6144], P(None, 'row'), may hold values from -0.21875 to 0.21875
- virt_irrep: int32 [64], replicated, may hold values from 0 to 7
- occ_irrep: int32 [96], replicated, may hold values from 0 to 7
- virt_energy: float32 [64], replicated, may hold values from 0.5 to 3
- occ_energy: float32 [96], replicated, may hold values from -3 to -0.5
Outputs:
- update: float32 [4096, 9216], P('row', 'col')
All inputs are finite; a program needn't handle non-finite values.
Results may differ from a plain program's by a relative error of at most 0.00005.
Values sent between devices are 32-bit elements; how exact they have to be, the bound alone decides.
No kernel may reach another device: no remote copies, remote signals or barrier semaphores. Data moves between devices by JAX's collectives and lax.ppermute only.
A program may use at most 192 MiB of HBM per device.

v0:
```python
import jax
import jax.numpy as jnp
from jax import lax
from jax.sharding import PartitionSpec as P


def pair_labels(first, second):
    return jnp.bitwise_xor(first[:, None], second[None, :]).reshape(-1)


def body(amps, ladder_ints, cycle_ints, virt_irrep, occ_irrep, virt_energy, occ_energy):
    highest = lax.Precision.HIGHEST
    row_count = lax.axis_size("row")
    col_count = lax.axis_size("col")
    row_index = lax.axis_index("row")
    col_index = lax.axis_index("col")
    virt_total = virt_irrep.shape[0]
    occ_total = occ_irrep.shape[0]
    virt_local = virt_total // row_count
    occ_local = occ_total // col_count
    virt_cols = virt_total // col_count
    pair_rows = amps.shape[0]
    virt_pairs = pair_labels(virt_irrep, virt_irrep)
    own_pairs = lax.dynamic_slice_in_dim(virt_pairs, row_index * pair_rows, pair_rows)
    rows_full = lax.all_gather(ladder_ints, "col", axis=1, tiled=True)
    masked = jnp.where(own_pairs[:, None] == virt_pairs[None, :], rows_full, jnp.float32(0.0))
    ladder = jnp.dot(
        masked,
        lax.all_gather(amps, "row", axis=0, tiled=True),
        precision=highest,
        preferred_element_type=jnp.float32,
    )
    blocks = amps.reshape(virt_local, virt_total, occ_local, occ_total)
    moved = lax.all_to_all(blocks, "col", split_axis=1, concat_axis=2, tiled=True)
    cycle_amps = moved.transpose(0, 2, 1, 3).reshape(virt_local * occ_total, virt_cols * occ_total)
    mixed_pairs = pair_labels(virt_irrep, occ_irrep)
    cycle_rows = cycle_amps.shape[0]
    own_mixed = lax.dynamic_slice_in_dim(mixed_pairs, row_index * cycle_rows, cycle_rows)
    part = cycle_ints
    part = jnp.where(mixed_pairs[:, None] == own_mixed[None, :], part, jnp.float32(0.0))
    cycle = lax.psum_scatter(
        jnp.dot(part, cycle_amps, precision=highest, preferred_element_type=jnp.float32),
        "row",
        scatter_dimension=0,
        tiled=True,
    )
    cycle_blocks = cycle.reshape(virt_local, occ_total, virt_cols, occ_total)
    returned = lax.all_to_all(cycle_blocks, "col", split_axis=1, concat_axis=2, tiled=True)
    cycle_back = returned.transpose(0, 2, 1, 3).reshape(
        virt_local * virt_total, occ_local * occ_total
    )
    own_virt = lax.dynamic_slice_in_dim(virt_energy, row_index * virt_local, virt_local)
    own_occ = lax.dynamic_slice_in_dim(occ_energy, col_index * occ_local, occ_local)
    row_energy = (own_virt[:, None] + virt_energy[None, :]).reshape(-1)
    col_energy = (own_occ[:, None] + occ_energy[None, :]).reshape(-1)
    return (ladder + cycle_back) / (row_energy[:, None] - col_energy[None, :])


def solution(mesh):
    placed = (P("row", "col"), P("row", "col"), P(None, "row"), P(), P(), P(), P())
    return jax.shard_map(
        body, mesh=mesh, in_specs=placed, out_specs=P("row", "col"), check_vma=False
    )
```

profile of v0, /device:TPU:0, one launch (start us, length us, event | category | flops | bytes accessed | tf_op | source)
XLA Modules:
  0.0 879.8 jit_solution(1245555769566114011)
XLA Ops:
  6.5 8.7 reshape.83
  15.2 9.7 %copy.14 = f32[16,64,12,96]{3,0,2,1:T(8,128)} copy(f32[16,64,12,96]{3,2,1,0:T(8,128)} %reshape.83) | data formatting | bytes 9437184 | tf_op jit(solution)/shard_map/reshape | solution.py:33
  24.9 6.5 all-to-all-start
  31.3 0.2 reduce-scatter.2.cloned.1.call-start
  31.7 0.1 xor.49
  31.8 0.1 dynamic_slice.13
  31.8 138.6 %all-to-all-done = f32[16,64,12,96]{3,0,2,1:T(8,128)} async-done(((f32[16,64,12,96]{3,0,2,1:T(8,128)}), f32[16,64,12,96]{3,0,2,1:T(8,128)}, u32[]{:S(2)}, u32[]{:S(2)}) %all-to-all-start) | async-done | bytes 4718624 | tf_op jit(solution)/shard_map/all_to_all | solution.py:34
  170.4 9.1 %copy.16 = f32[16,8,8,12,96]{4,1,3,2,0:T(8,128)} copy(f32[16,8,8,12,96]{4,0,3,1,2:T(8,128)} %bitcast.2) | data formatting | bytes 9437184 | tf_op jit(solution)/shard_map/all_to_all | solution.py:34
  179.5 7.4 reshape.84
  186.8 108.4 %fusion = f32[6144,768]{1,0:T(8,128)} fusion(f32[1536,768]{1,0:T(8,128)} %reshape.84, f32[6144,1536]{1,0:T(8,128)} %param.9, s32[1536]{0:T(1024)S(1)} %dynamic_slice.13, s32[6144]{0:T(1024)S(1)} %xor.49), kind=kOutput, calls=%fused_computation | convolution fusion | flops 86991962112 | bytes 61372416 | tf_op jit(solution)/shard_map/dot_general | solution.py:42
  295.3 0.7 all-gather.5.cloned.1.call-update
  296.1 0.7 all-gather.3.cloned.1.call-update
  296.8 168.5 %reduce-scatter.2.cloned.1.call-done = f32[1536,768]{1,0:T(8,128)} async-done(((f32[6144,768]{1,0:T(8,128)}), f32[1536,768]{1,0:T(8,128)}) %reduce-scatter.2.cloned.1.call-update) | async-done | bytes 4718608 | tf_op jit(solution)/shard_map/reduce_scatter | solution.py:41
  465.2 7.7 reshape.85
  472.9 8.1 copy.17
  481.1 5.3 all-to-all-start.1
  486.5 0.1 xor.45
  486.8 0.1 dynamic_slice.15
  486.9 0.1 add.69
  487.0 138.1 %all-to-all-done.1 = f32[16,96,8,96]{3,2,0,1:T(8,128)} async-done(((f32[16,96,8,96]{3,2,0,1:T(8,128)}), f32[16,96,8,96]{3,2,0,1:T(8,128)}, u32[]{:S(2)}, u32[]{:S(2)}) %all-to-all-start.1) | async-done | bytes 4718624 | tf_op jit(solution)/shard_map/all_to_all | solution.py:48
  625.1 9.8 %copy.18 = f32[16,12,8,8,96]{4,1,3,2,0:T(8,128)} copy(f32[16,12,8,8,96]{4,3,0,1,2:T(8,128)} %bitcast.6) | data formatting | bytes 9437184 | tf_op jit(solution)/shard_map/all_to_all | solution.py:48
  634.9 8.4 reshape.86
  643.3 152.8 %all-gather.3.cloned.1.call-done = f32[1024,4096]{1,0:T(8,128)} async-done(((f32[1024,512]{1,0:T(8,128)}), f32[1024,4096]{1,0:T(8,128)}) %all-gather.3.cloned.1.call-update) | async-done | bytes 16777232 | tf_op jit(solution)/shard_map/all_gather | solution.py:25
  796.0 77.2 %subtract_divide_fusion = f32[1024,1152]{1,0:T(8,128)} fusion(f32[1024,1152]{1,0:T(8,128)} %reshape.86, f32[4096,1152]{1,0:T(8,128)} %all-gather.5.cloned.1.call-done, f32[1024,4096]{1,0:T(8,128)} %all-gather.3.cloned.1.call-done, s32[4096]{0:T(1024)S(1)} %xor.45, s32[1024]{0:T(1024)S(1)} %dynamic_slice.12, f32[1152]{0:T(1024)S(1)} %add.69, f32[1024]{0:T(1024)S(1)} %add.64), kind=kOutput, calls=%fused_computation.12 | convolution fusion | flops 57993986048 | bytes 45117952 | tf_op jit(solution)/shard_map/dot_general | solution.py:27
  (19 shorter events, 0.6 us)
Async XLA Ops:
  24.9 6.7 copy-start
  24.9 6.7 copy-start.1
  24.9 145.5 %all-to-all-start = ((f32[16,64,12,96]{3,0,2,1:T(8,128)}), f32[16,64,12,96]{3,0,2,1:T(8,128)}, u32[]{:S(2)}, u32[]{:S(2)}) async-start(f32[16,64,12,96]{3,0,2,1:T(8,128)} %copy.14), calls=%async_computation | async-start | bytes 12582912 | tf_op jit(solution)/shard_map/all_to_all | solution.py:34
  31.3 433.9 %reduce-scatter.2.cloned.1.call-start = ((), (), s32[]{:S(2)}) async-start(), calls=%async_computation.5 | async-start | bytes 23592960 | tf_op jit(solution)/shard_map/reduce_scatter | solution.py:41
  295.3 348.0 %all-gather.5.cloned.1.call-start = ((), (), s32[]{:S(2)}) async-start(), calls=%async_computation.4 | async-start | bytes 23592960 | tf_op jit(solution)/shard_map/all_gather | solution.py:29
  296.0 500.0 %all-gather.3.cloned.1.call-start = ((), (), s32[]{:S(2)}) async-start(), calls=%async_computation.3 | async-start | bytes 18874368 | tf_op jit(solution)/shard_map/all_gather | solution.py:25
  481.1 5.5 copy-start.2
  481.1 5.7 copy-start.3
  481.1 144.1 %all-to-all-start.1 = ((f32[16,96,8,96]{3,2,0,1:T(8,128)}), f32[16,96,8,96]{3,2,0,1:T(8,128)}, u32[]{:S(2)}, u32[]{:S(2)}) async-start(f32[16,96,8,96]{3,2,0,1:T(8,128)} %copy.17), calls=%async_computation.2 | async-start | bytes 12582912 | tf_op jit(solution)/shard_map/all_to_all | solution.py:48
Sparse Core Ops, SparseCore 0:
  295.4 169.7 reduce-scatter.1
  467.2 175.8 all-gather.4
  644.9 151.0 all-gather.2
where the time goes:
time: 881 us; the launch traced here: 880 us
  waiting for transfers between devices  599 us (68%)
  matrix products  186 us (21%)
  local copies, waits for them, and re-layouts  69.3 us (8%)
  between operations  13.2 us (1%)
  starting transfers between devices  12.1 us (1%)
    reduce_scatter x1, waiting for transfers between devices, body(): lax.psum_scatter(jnp.dot(part, cycle_amps, precision=highest, preferred_e...  168 us
    all_gather x1, waiting for transfers between devices, body(): rows_full = lax.all_gather(ladder_ints, 'col', axis=1, tiled=True)  153 us
    all_to_all x1, waiting for transfers between devices, body(): lax.all_to_all(blocks, 'col', split_axis=1, concat_axis=2, tiled=True)  139 us
    all_to_all x1, waiting for transfers between devices, body(): lax.all_to_all(cycle_blocks, 'col', split_axis=1, concat_axis=2, tiled=True)  138 us
    dot_general x1, matrix products, body(): jnp.dot(part, cycle_amps, precision=highest, preferred_element_type=jnp.f...  108 us
    dot_general x1, matrix products, body(): jnp.dot(masked, lax.all_gather(amps, 'row', axis=0, tiled=True), precisio...  77.2 us
    reshape x2, local copies, waits for them, and re-layouts, body(): blocks = amps.reshape(virt_local, virt_total, occ_local, occ_total)  18.3 us
  transfers between devices with their start and end apart: 5, of which 4 were waited for; matrix products, arithmetic and copies ran while one was open for 4% of the time, Pallas kernels for 0%

commit v1 on v0

--- a/solution.py
+++ b/solution.py
@@ -1,15 +1,451 @@
+import functools
+
 import jax
 import jax.numpy as jnp
 from jax import lax
+from jax.experimental import pallas as pl
+from jax.experimental.pallas import tpu as pltpu
 from jax.sharding import PartitionSpec as P
+
+PARTS = 4
+WINDOW = 128
+TILE = 256
+SMALL = pl.CostEstimate(flops=0, bytes_accessed=0, transcendentals=0)
+PARAMS = pltpu.CompilerParams(vmem_limit_bytes=56 * 1024 * 1024)
 
 
 def pair_labels(first, second):
     return jnp.bitwise_xor(first[:, None], second[None, :]).reshape(-1)
 
 
+def halves(value):
+    high = value.astype(jnp.bfloat16)
+    return high, (value - high.astype(jnp.float32)).astype(jnp.bfloat16)
+
+
+def dot(left, right):
+    return jnp.dot(left, right, preferred_element_type=jnp.float32)
+
+
+def to_cycle_kernel(occ, depth, moved_ref, high_ref, low_ref, cells, rows):
+    _, height, width = moved_ref.shape
+    sources, count = height // depth, width // occ
+    for source in range(sources):
+        value = moved_ref[0, source * depth : (source + 1) * depth, :]
+        for k in range(count):
+            at = (source * count + k) * 8
+            cells[at : at + depth, 0:occ] = value[:, k * occ : (k + 1) * occ]
+    for d in range(depth):
+        value = cells[pl.ds(d, sources * count, stride=8), :]
+        rows[:, d * occ : (d + 1) * occ] = value[:, 0:occ]
+    high, low = halves(rows[...])
+    high_ref[...] = high
+    low_ref[...] = low
+
+
+def to_cycle_rows(moved, occ):
+    count, sources, depth, width = moved.shape
+    height = sources * width // occ
+    shape = jax.ShapeDtypeStruct((count * height, depth * occ), jnp.bfloat16)
+    return pl.pallas_call(
+        functools.partial(to_cycle_kernel, occ, depth),
+        grid=(count,),
+        in_specs=[pl.BlockSpec((1, sources * depth, width), lambda c: (c, 0, 0))],
+        out_specs=[pl.BlockSpec((height, depth * occ), lambda c: (c, 0))] * 2,
+        out_shape=[shape, shape],
+        scratch_shapes=[
+            pltpu.VMEM((height * 8, 128), jnp.float32),
+            pltpu.VMEM((height, depth * occ), jnp.float32),
+        ],
+        compiler_params=PARAMS,
+        cost_estimate=SMALL,
+        name="to_cycle_rows",
+    )(moved.reshape(count, sources * depth, width))
+
+
+def cycle_kernel(
+    base, ints_ref, rows_ref, own_ref, high_0, low_0, high_1, low_1, send_y, send_x, keep_y, keep_x
+):
+    step = pl.program_id(0)
+    masked = jnp.where(rows_ref[...] == own_ref[...], ints_ref[...], jnp.float32(0.0))
+    high, low = halves(masked)
+    middle = high_0.shape[0]
+    total = dot(low[:, :middle], high_0[...]) + dot(low[:, middle:], high_1[...])
+    total += dot(high[:, :middle], low_0[...]) + dot(high[:, middle:], low_1[...])
+    total += dot(high[:, :middle], high_0[...]) + dot(high[:, middle:], high_1[...])
+    half = total.shape[0] // 2
+
+    @pl.when(step < 2)
+    def _():
+        send_y[0] = total[:half]
+
+    @pl.when(step >= 2)
+    def _():
+        keep_y[0] = total[:half]
+
+    @pl.when(step % 2 == 0)
+    def _():
+        send_x[0] = total[half:]
+
+    @pl.when(step % 2 == 1)
+    def _():
+        keep_x[0] = total[half:]
+
+
+def cycle_sums(part, row_index, ints, labels, own_labels, rights):
+    depth = ints.shape[1]
+    width = rights[0].shape[1]
+    height = ints.shape[0] // 4 // PARTS
+    base = jnp.reshape(row_index, (1,)).astype(jnp.int32)
+
+    def at(step, base):
+        return (base[0] ^ (3 - step)) * PARTS + part, 0
+
+    def still(step, base):
+        return 0, 0
+
+    shape = jax.ShapeDtypeStruct((2, height // 2, width), jnp.float32)
+    block = (1, height // 2, width)
+    return pl.pallas_call(
+        cycle_kernel,
+        grid_spec=pltpu.PrefetchScalarGridSpec(
+            num_scalar_prefetch=1,
+            grid=(4,),
+            in_specs=[
+                pl.BlockSpec((height, depth), at),
+                pl.BlockSpec((height, 1), at),
+                pl.BlockSpec((1, depth), still),
+            ]
+            + [pl.BlockSpec(value.shape, still) for value in rights],
+            out_specs=[
+                pl.BlockSpec(block, lambda step, base: (jnp.where(step == 0, 1, 0), 0, 0)),
+                pl.BlockSpec(block, lambda step, base: (jnp.where(step < 2, 1, 0), 0, 0)),
+                pl.BlockSpec(block, lambda step, base: (jnp.where(step < 3, 1, 0), 0, 0)),
+                pl.BlockSpec(block, lambda step, base: (jnp.where(step < 2, 1, 0), 0, 0)),
+            ],
+        ),
+        out_shape=[shape] * 4,
+        compiler_params=PARAMS,
+        cost_estimate=SMALL,
+        name="cycle_sums",
+    )(base, ints, labels, own_labels, *rights)
+
+
+def owner_kernel(occ_local, *refs):
+    *values, out_ref = refs
+    count, rows, _ = out_ref.shape
+    virt = rows // occ_local
+    for half in range(2):
+        keep, near, far = values[half * 3 : half * 3 + 3]
+        total = keep[0] + near[0] + far[0]
+        for a in range(virt // 2):
+            for target in range(count):
+                begin = (a * count + target) * occ_local
+                at = (half * virt // 2 + a) * occ_local
+                out_ref[target, at : at + occ_local, :] = total[begin : begin + occ_local, :]
+
+
+def owner_blocks(low, high, count, occ_local):
+    _, height, width = low[0].shape
+    rows = 2 * height // count
+    return pl.pallas_call(
+        functools.partial(owner_kernel, occ_local),
+        grid=(1,),
+        in_specs=[pl.BlockSpec((1, height, width), lambda step: (0, 0, 0))] * 6,
+        out_specs=pl.BlockSpec((count, rows, width), lambda step: (0, 0, 0)),
+        out_shape=jax.ShapeDtypeStruct((count, rows, width), jnp.float32),
+        compiler_params=PARAMS,
+        cost_estimate=SMALL,
+        name="owner_blocks",
+    )(*low, *high)
+
+
+def update_kernel(occ, occ_local, at, back_ref, ladder_ref, rows_ref, cols_ref, out_ref, cells, rows):
+    sources, height, width = back_ref.shape
+    count = width // occ
+    pad = -(-occ_local // 8) * 8
+    for a in range(height // occ_local):
+        for source in range(sources):
+            value = back_ref[source, a * occ_local : (a + 1) * occ_local, :]
+            for b in range(count):
+                at = ((a * sources + source) * count + b) * pad
+                cells[at : at + occ_local, 0:occ] = value[:, b * occ : (b + 1) * occ]
+    for i in range(occ_local):
+        value = cells[pl.ds(i, rows.shape[0], stride=pad), :]
+        rows[:, i * occ : (i + 1) * occ] = value[:, 0:occ]
+    out_ref[...] = (ladder_ref[...] + rows[...]) / (rows_ref[...] - cols_ref[...])
+
+
+def with_cycle(part, back, ladder, row_energy, col_energy, occ, occ_local):
+    sources, rows, width = back.shape
+    columns = ladder.shape[1]
+    height = rows // occ_local * sources * width // occ
+    pad = -(-occ_local // 8) * 8
+    block = pl.BlockSpec((height, columns), lambda step, at: (at[0], 0))
+    return pl.pallas_call(
+        functools.partial(update_kernel, occ, occ_local),
+        grid_spec=pltpu.PrefetchScalarGridSpec(
+            num_scalar_prefetch=1,
+            grid=(1,),
+            in_specs=[
+                pl.BlockSpec(back.shape, lambda step, at: (0, 0, 0)),
+                block,
+                pl.BlockSpec((height, 1), lambda step, at: (0, 0)),
+                pl.BlockSpec((1, columns), lambda step, at: (0, 0)),
+            ],
+            out_specs=block,
+            scratch_shapes=[
+                pltpu.VMEM((height * pad, 128), jnp.float32),
+                pltpu.VMEM((height, columns), jnp.float32),
+            ],
+        ),
+        out_shape=jax.ShapeDtypeStruct(ladder.shape, jnp.float32),
+        input_output_aliases={2: 0},
+        compiler_params=PARAMS,
+        cost_estimate=SMALL,
+        name="with_cycle",
+    )(
+        jnp.full((1,), part, jnp.int32),
+        back,
+        ladder,
+        row_energy[part * height : (part + 1) * height],
+        col_energy,
+    )
+
+
+def ladder_kernel(fresh, start, packed_ref, rank_ref, label_ref, own_ref, amps_ref, *refs):
+    total_ref, (out_ref, high_ref, low_ref) = (None, refs) if fresh else (refs[0], refs[1:])
+
+    @pl.when(pl.program_id(0) == 0)
+    def _():
+        high, low = halves(amps_ref[...])
+        high_ref[...] = high
+        low_ref[...] = low
+
+    size, tile, window = packed_ref.shape
+    wide = rank_ref.shape[2]
+    total = None if fresh else total_ref[...]
+    for n in range(size):
+        pick = lax.broadcasted_iota(jnp.int32, (window, wide), 0) == rank_ref[n]
+        pick = pick.astype(jnp.float32).astype(jnp.bfloat16)
+        high, low = halves(packed_ref[n])
+        ints = dot(high, pick) + dot(low, pick)
+        ints = jnp.where(own_ref[...] == label_ref[n], ints, jnp.float32(0.0))
+        high, low = halves(ints)
+        at = slice(n * wide, (n + 1) * wide)
+        term = dot(low, high_ref[at, :]) + dot(high, low_ref[at, :]) + dot(high, high_ref[at, :])
+        total = term if total is None else total + term
+    out_ref[...] = total
+
+
+def ladder_term(start, packed, ranks, labels, own_pairs, amps, total=None):
+    blocks, rows, window = packed.shape
+    wide = ranks.shape[2]
+    depth, columns = amps.shape
+    size = depth // wide
+    fresh = total is None
+    out_block = pl.BlockSpec((TILE, columns), lambda m, start: (m, 0))
+    small = pl.BlockSpec((size, 1, wide), lambda m, start: (start[0], 0, 0))
+    return pl.pallas_call(
+        functools.partial(ladder_kernel, fresh),
+        grid_spec=pltpu.PrefetchScalarGridSpec(
+            num_scalar_prefetch=1,
+            grid=(rows // TILE,),
+            in_specs=[
+                pl.BlockSpec((size, TILE, window), lambda m, start: (start[0], m, 0)),
+                small,
+                small,
+                pl.BlockSpec((TILE, 1), lambda m, start: (m, 0)),
+                pl.BlockSpec((depth, columns), lambda m, start: (0, 0)),
+            ]
+            + ([] if fresh else [out_block]),
+            out_specs=out_block,
+            scratch_shapes=[pltpu.VMEM((depth, columns), jnp.bfloat16)] * 2,
+        ),
+        out_shape=jax.ShapeDtypeStruct((rows, columns), jnp.float32),
+        input_output_aliases={} if fresh else {6: 0},
+        compiler_params=PARAMS,
+        cost_estimate=SMALL,
+        name="ladder_term",
+    )(
+        jnp.reshape(start // size, (1,)).astype(jnp.int32),
+        packed,
+        ranks,
+        labels,
+        own_pairs,
+        amps,
+        *([] if fresh else [total]),
+    )
+
+
 def body(amps, ladder_ints, cycle_ints, virt_irrep, occ_irrep, virt_energy, occ_energy):
-    highest = lax.Precision.HIGHEST
+    row_count = lax.axis_size("row")
+    col_count = lax.axis_size("col")
+    row_index = lax.axis_index("row")
+    col_index = lax.axis_index("col")
+    virt_total = virt_irrep.shape[0]
+    occ_total = occ_irrep.shape[0]
+    virt_local = virt_total // row_count
+    occ_local = occ_total // col_count
+    virt_cols = virt_total // col_count
+    pair_rows, columns = amps.shape
+    ladder_cols = ladder_ints.shape[1]
+    virt_pairs = pair_labels(virt_irrep, virt_irrep)
+    own_pairs = lax.dynamic_slice_in_dim(virt_pairs, row_index * pair_rows, pair_rows)
+    mixed_pairs = pair_labels(virt_irrep, occ_irrep)
+    cycle_rows = virt_local * occ_total
+    own_mixed = lax.dynamic_slice_in_dim(mixed_pairs, row_index * cycle_rows, cycle_rows)
+    barrier = lax.optimization_barrier
+
+    def swap(value, flip):
+        return lax.ppermute(value, "row", [(i, i ^ flip) for i in range(row_count)])
+
+    half_virt = virt_local // 2
+    half_rows = pair_rows // 2
+    first, second = amps[:half_rows], amps[half_rows:]
+
+    def to_cycle(value):
+        blocks = value.reshape(half_virt, col_count, virt_cols, columns)
+        return lax.all_to_all(blocks, "col", split_axis=1, concat_axis=1, tiled=True)
+
+    first_2, second_1 = swap(first, 2), swap(second, 1)
+    moved = to_cycle(first)
+    held_first, held, first_2, second_1, moved = barrier((first, second, first_2, second_1, moved))
+    first_1, second_2 = swap(held_first, 1), swap(held, 2)
+    rights = to_cycle_rows(moved, occ_total)
+    moved = to_cycle(held)
+    moved, first_1, second_2, first_2, second_1 = barrier(
+        (moved, first_1, second_2, first_2, second_1)
+    )
+    first_3, second_3 = swap(first_2, 1), swap(second_1, 2)
+    rights = rights + to_cycle_rows(moved, occ_total)
+
+    blocks = virt_pairs.reshape(col_count, ladder_cols)
+    place = jnp.arange(ladder_cols)
+    same = (blocks[:, :, None] == blocks[:, None, :]) & (place[None, None, :] < place[None, :, None])
+    rank = jnp.sum(same, axis=2, dtype=jnp.int32)
+    turns = jnp.max(rank) // WINDOW + 1
+    own_rank = lax.dynamic_index_in_dim(rank, col_index, 0, keepdims=False)
+    own_block = lax.dynamic_index_in_dim(blocks, col_index, 0, keepdims=False)
+    masked_ints = jnp.where(own_pairs[:, None] == own_block[None, :], ladder_ints, jnp.float32(0.0))
+
+    def packed_ints(turn):
+        pick = own_rank[:, None] == turn * WINDOW + jnp.arange(WINDOW)[None, :]
+        return jnp.dot(
+            masked_ints,
+            pick.astype(jnp.float32),
+            precision=lax.Precision.HIGH,
+            preferred_element_type=jnp.float32,
+        )
+
+    def gathered(packed):
+        return lax.all_gather(packed, "col", axis=0, tiled=False)
+
+    def ladder_from(packed, turn, pieces, total=None):
+        for flip, half, value in pieces:
+            start = (row_index ^ flip) * (pair_rows // ladder_cols)
+            start += half * (half_rows // ladder_cols)
+            total = ladder_term(
+                start,
+                packed,
+                rank[:, None, :] - turn * WINDOW,
+                blocks[:, None, :],
+                own_pairs[:, None],
+                value,
+                total,
+            )
+        return total
+
+    packed, rights = barrier((packed_ints(0), rights))
+    packed = gathered(packed)
+
+    own_virt = lax.dynamic_slice_in_dim(virt_energy, row_index * virt_local, virt_local)
+    own_occ = lax.dynamic_slice_in_dim(occ_energy, col_index * occ_local, occ_local)
+    row_energy = (own_virt[:, None] + virt_energy[None, :]).reshape(-1)[:, None]
+    col_energy = (own_occ[:, None] + occ_energy[None, :]).reshape(-1)[None, :]
+
+    sums = functools.partial(
+        cycle_sums, row_index=row_index, ints=cycle_ints, labels=mixed_pairs[:, None],
+        own_labels=own_mixed[None, :],
+    )
+    def pass_on(keep, near):
+        return swap(keep[0][1:] + near[0][1:], 1), swap(keep[1][1:] + near[1][1:], 2)
+
+    def send(values):
+        return swap(values[0], 2), swap(values[1], 1)
+
+    def owned(keep, near, far):
+        return owner_blocks(
+            (keep[0], near[0], far[0]), (keep[1], near[1], far[1]), col_count, occ_local
+        )
+
+    def to_owner(blocks):
+        return lax.all_to_all(blocks, "col", split_axis=0, concat_axis=0, tiled=True)
+
+    def part_sums(part, rights):
+        values = sums(part, rights=rights)
+        return values[:2], values[2:]
+
+    pieces = [(0, 0, first), (0, 1, second), (2, 0, first_2), (1, 1, second_1)]
+    pieces += [(1, 0, first_1), (2, 1, second_2)]
+    out_0, keep_0 = part_sums(0, rights)
+    near_0 = send(out_0)
+    rights, keep_0 = barrier((rights, keep_0))
+    out_1, keep_1 = part_sums(1, rights)
+
+    rights, first_3, second_3, near_0, keep_0, out_1, keep_1 = barrier(
+        (rights, first_3, second_3, near_0, keep_0, out_1, keep_1)
+    )
+    pieces += [(3, 0, first_3), (3, 1, second_3)]
+    far_0, near_1 = pass_on(keep_0, near_0), send(out_1)
+    out_2, keep_2 = part_sums(2, rights)
+    packed, keep_2 = barrier((packed, keep_2))
+    ladder = ladder_from(packed, 0, pieces[:2])
+
+    rights, ladder, far_0, near_0, keep_0, near_1, keep_1, out_2, keep_2 = barrier(
+        (rights, ladder, far_0, near_0, keep_0, near_1, keep_1, out_2, keep_2)
+    )
+    far_1, near_2 = pass_on(keep_1, near_1), send(out_2)
+    back_0 = to_owner(owned(keep_0, near_0, far_0))
+    out_3, keep_3 = part_sums(3, rights)
+    ladder, keep_3 = barrier((ladder, keep_3))
+    ladder = ladder_from(packed, 0, pieces[2:4], ladder)
+
+    ladder, back_0, far_1, near_1, keep_1, near_2, keep_2, out_3, keep_3 = barrier(
+        (ladder, back_0, far_1, near_1, keep_1, near_2, keep_2, out_3, keep_3)
+    )
+    far_2, near_3 = pass_on(keep_2, near_2), send(out_3)
+    back_1 = to_owner(owned(keep_1, near_1, far_1))
+    ladder = ladder_from(packed, 0, pieces[4:7], ladder)
+
+    ladder, back_1, far_2, near_2, keep_2, near_3, keep_3 = barrier(
+        (ladder, back_1, far_2, near_2, keep_2, near_3, keep_3)
+    )
+    far_3 = pass_on(keep_3, near_3)
+    back_2 = to_owner(owned(keep_2, near_2, far_2))
+    ladder = ladder_from(packed, 0, pieces[7:], ladder)
+
+    ladder, back_2, far_3, near_3, keep_3 = barrier((ladder, back_2, far_3, near_3, keep_3))
+    back_3 = to_owner(owned(keep_3, near_3, far_3))
+    backs = [back_0, back_1, back_2, back_3]
+    update = ladder
+    for part in range(PARTS):
+        update = with_cycle(
+            part, backs[part], update, row_energy, col_energy, occ_total, occ_local
+        )
+    return lax.fori_loop(
+        1,
+        turns,
+        lambda turn, total: total
+        + ladder_from(gathered(packed_ints(turn)), turn, pieces) / (row_energy - col_energy),
+        update,
+    )
+
+
+def plain_body(
+    amps, ladder_ints, cycle_ints, virt_irrep, occ_irrep, virt_energy, occ_energy
+):
+    high = lax.Precision.HIGH
     row_count = lax.axis_size("row")
     col_count = lax.axis_size("col")
     row_index = lax.axis_index("row")
@@ -27,7 +463,7 @@
     ladder = jnp.dot(
         masked,
         lax.all_gather(amps, "row", axis=0, tiled=True),
-        precision=highest,
+        precision=high,
         preferred_element_type=jnp.float32,
     )
     blocks = amps.reshape(virt_local, virt_total, occ_local, occ_total)
@@ -39,7 +475,7 @@
     part = cycle_ints
     part = jnp.where(mixed_pairs[:, None] == own_mixed[None, :], part, jnp.float32(0.0))
     cycle = lax.psum_scatter(
-        jnp.dot(part, cycle_amps, precision=highest, preferred_element_type=jnp.float32),
+        jnp.dot(part, cycle_amps, precision=high, preferred_element_type=jnp.float32),
         "row",
         scatter_dimension=0,
         tiled=True,
@@ -58,6 +494,7 @@
 
 def solution(mesh):
     placed = (P("row", "col"), P("row", "col"), P(None, "row"), P(), P(), P(), P())
+    plan = body if mesh.shape["row"] == 4 else plain_body
     return jax.shard_map(
-        body, mesh=mesh, in_specs=placed, out_specs=P("row", "col"), check_vma=False
-    )
+        plan, mesh=mesh, in_specs=placed, out_specs=P("row", "col"), check_vma=False
+    )

time: 881 us -> 482 us (0.55)
  waiting for transfers between devices: 599 us -> 149 us
  Pallas kernels: 0 us -> 205 us
  matrix products: 186 us -> 1.57 us
  starting transfers between devices: 12.1 us -> 53 us
  local copies, waits for them, and re-layouts: 69.3 us -> 33.2 us
  other arithmetic: 0.29 us -> 18.8 us
    all_to_all x2 -> x6, waiting for transfers between devices: 277 us -> 19.1 us  [the longest x4 18.9 us: to_owner(): lax.all_to_all(blocks, 'col', split_axis=0, concat_axis=0, tiled=True)]
    pallas_call x0 -> x22, Pallas kernels: none -> 205 us  [the longest x4 83.1 us: cycle_sums(): pl.pallas_call(cycle_kernel, grid_spec=pltpu.PrefetchScalarGridSpec(num_s...]
    dot_general x2 -> x1, matrix products: 186 us -> 1.57 us  [packed_ints(): jnp.dot(masked_ints, pick.astype(jnp.float32), precision=lax.Precision.HI...]
    reduce_scatter x1 -> x0, waiting for transfers between devices: 168 us -> none  [body(): lax.psum_scatter(jnp.dot(part, cycle_amps, precision=highest, preferred_e...]
    all_gather x2 -> x1, waiting for transfers between devices: 153 us -> 0.01 us  [gathered(): return lax.all_gather(packed, 'col', axis=0, tiled=False)]
    ppermute x0 -> x22, waiting for transfers between devices: none -> 129 us  [swap(): return lax.ppermute(value, 'row', [(i, i ^ flip) for i in range(row_count)])]
    reshape x6 -> x2, local copies, waits for them, and re-layouts: 49.9 us -> 3.13 us  [to_cycle(): blocks = value.reshape(half_virt, col_count, virt_cols, columns)]
    ppermute x0 -> x22, starting transfers between devices: none -> 23.6 us  [swap(): return lax.ppermute(value, 'row', [(i, i ^ flip) for i in range(row_count)])]
  transfers between devices with their start and end apart: 5 -> 29, of which waited for: 4 -> 12; matrix products, arithmetic and copies ran while one was open for 4% -> 8% of each run, Pallas kernels for 0% -> 38%
where the time goes in v1:
time: 482 us; the launch traced here: 477 us
  Pallas kernels  205 us (43%)
  waiting for transfers between devices  149 us (31%)
  starting transfers between devices  53 us (11%)
  local copies, waits for them, and re-layouts  33.2 us (7%)
  other arithmetic  18.8 us (4%)
  between operations  16.2 us (3%)
    ppermute x22, waiting for transfers between devices, swap(): return lax.ppermute(value, 'row', [(i, i ^ flip) for i in range(row_count)])  129 us
    pallas_call x4, Pallas kernels, cycle_sums(): pl.pallas_call(cycle_kernel, grid_spec=pltpu.PrefetchScalarGridSpec(num_s...  83.1 us
    pallas_call x8, Pallas kernels, ladder_term(): pl.pallas_call(functools.partial(ladder_kernel, fresh), grid_spec=pltpu.P...  77.1 us
    ppermute x22, starting transfers between devices, swap(): return lax.ppermute(value, 'row', [(i, i ^ flip) for i in range(row_count)])  23.6 us
    all_to_all x4, waiting for transfers between devices, to_owner(): lax.all_to_all(blocks, 'col', split_axis=0, concat_axis=0, tiled=True)  18.9 us
    all_to_all x4, starting transfers between devices, to_owner(): lax.all_to_all(blocks, 'col', split_axis=0, concat_axis=0, tiled=True)  18.2 us
    pallas_call x4, Pallas kernels, with_cycle(): pl.pallas_call(functools.partial(update_kernel, occ, occ_local), grid_spe...  16.5 us
    pallas_call x2, Pallas kernels, to_cycle_rows(): pl.pallas_call(functools.partial(to_cycle_kernel, occ, depth), grid=(coun...  14.4 us
  transfers between devices with their start and end apart: 29, of which 12 were waited for; matrix products, arithmetic and copies ran while one was open for 8% of the time, Pallas kernels for 38%

profile of v1, /device:TPU:0, one launch (start us, length us, event | category | flops | bytes accessed | tf_op | source)
XLA Modules:
  0.0 477.0 jit_solution(6615875477548617688)
XLA Ops:
  12.3 6.3 %all-to-all-start = ((f32[8,8,8,1152]{3,2,0,1:T(8,128)}), f32[8,8,8,1152]{3,2,0,1:T(8,128)}, u32[]{:S(2)}, u32[]{:S(2)}) async-start(f32[8,8,8,1152]{3,2,0,1:T(8,128)} %copy.90), calls=%async_computation | async-start | bytes 4718592 | tf_op jit(solution)/shard_map/all_to_all | solution.py:309
  21.6 51.0 %collective-permute-done.amps_ref = f32[512,1152]{1,0:T(8,128)} collective-permute-done((f32[512,1152]{1,0:T(8,128)}, f32[512,1152]{1,0:T(8,128)}, u32[]{:S(2)}, u32[]{:S(2)}) %collective-permute-start) | collective-permute-done | bytes 2359328 | tf_op jit(solution)/shard_map/ppermute | solution.py:301
  75.2 4.9 %all-to-all-start.1 = ((f32[8,8,8,1152]{3,2,0,1:T(8,128)}), f32[8,8,8,1152]{3,2,0,1:T(8,128)}, u32[]{:S(2)}, u32[]{:S(2)}) async-start(f32[8,8,8,1152]{3,2,0,1:T(8,128)} %copy.92), calls=%async_computation.1 | async-start | bytes 4718592 | tf_op jit(solution)/shard_map/all_to_all | solution.py:309
  93.9 7.2 %to_cycle_rows.2 = (bf16[768,768]{1,0:T(8,128)(2,1)}, bf16[768,768]{1,0:T(8,128)(2,1)}) custom-call(f32[8,64,1152]{2,1,0:T(8,128)} %bitcast.77), custom_call_target="tpu_custom_call" | custom-call | tf_op jit(solution)/shard_map/to_cycle_rows/pallas_call | solution.py:50
  101.2 32.7 %collective-permute-done.3.amps_ref = f32[512,1152]{1,0:T(8,128)} collective-permute-done((f32[512,1152]{1,0:T(8,128)S(1)}, f32[512,1152]{1,0:T(8,128)}, u32[]{:S(2)}, u32[]{:S(2)}) %collective-permute-start.3) | collective-permute-done | bytes 2359328 | tf_op jit(solution)/shard_map/ppermute | solution.py:301
  138.1 7.2 %to_cycle_rows.3 = (bf16[768,768]{1,0:T(8,128)(2,1)}, bf16[768,768]{1,0:T(8,128)(2,1)}) custom-call(f32[8,64,1152]{2,1,0:T(8,128)} %bitcast.78), custom_call_target="tpu_custom_call" | custom-call | tf_op jit(solution)/shard_map/to_cycle_rows/pallas_call | solution.py:50
  148.0 4.8 xor.135.rows_ref
  153.4 17.8 %cycle_sums.4 = (f32[2,192,768]{2,1,0:T(8,128)}, f32[2,192,768]{2,1,0:T(8,128)}, f32[2,192,768]{2,1,0:T(8,128)}, f32[2,192,768]{2,1,0:T(8,128)}) custom-call(s32[1]{0:T(128)} %bitcast.8.base, f32[6144,1536]{1,0:T(8,128)} %ints_ref.7, s32[6144,1]{1,0:T(8,128)} %xor.135.rows_ref, s32[1,1536]{1,0:T(1,128)} %broadcast_in_dim.13.own_ref, ...), custom_call_target="tpu_custom_call" | custom-call | tf_op jit(solution)/shard_map/cycle_sums/pallas_call | solution.py:109
  173.2 17.6 %cycle_sums.5 = (f32[2,192,768]{2,1,0:T(8,128)}, f32[2,192,768]{2,1,0:T(8,128)}, f32[2,192,768]{2,1,0:T(8,128)}, f32[2,192,768]{2,1,0:T(8,128)}) custom-call(s32[1]{0:T(128)} %bitcast.8.base, f32[6144,1536]{1,0:T(8,128)} %ints_ref.7, s32[6144,1]{1,0:T(8,128)} %xor.135.rows_ref, s32[1,1536]{1,0:T(1,128)} %broadcast_in_dim.13.own_ref, ...), custom_call_target="tpu_custom_call" | custom-call | tf_op jit(solution)/shard_map/cycle_sums/pallas_call | solution.py:109
  190.8 34.1 %collective-permute-done.6.refs_1_ = f32[2,192,768]{2,1,0:T(8,128)S(1)} collective-permute-done((f32[2,192,768]{2,1,0:T(8,128)}, f32[2,192,768]{2,1,0:T(8,128)S(1)}, u32[]{:S(2)}, u32[]{:S(2)}) %collective-permute-start.6) | collective-permute-done | bytes 1179680 | tf_op jit(solution)/shard_map/ppermute | solution.py:301
  235.9 30.1 %cycle_sums.6 = (f32[2,192,768]{2,1,0:T(8,128)}, f32[2,192,768]{2,1,0:T(8,128)}, f32[2,192,768]{2,1,0:T(8,128)}, f32[2,192,768]{2,1,0:T(8,128)}) custom-call(s32[1]{0:T(128)} %bitcast.8.base, f32[6144,1536]{1,0:T(8,128)} %ints_ref.7, s32[6144,1]{1,0:T(8,128)} %xor.135.rows_ref, s32[1,1536]{1,0:T(1,128)} %broadcast_in_dim.13.own_ref, ...), custom_call_target="tpu_custom_call" | custom-call | tf_op jit(solution)/shard_map/cycle_sums/pallas_call | solution.py:109
  266.0 9.1 %ladder_term.20.refs_0_ = f32[1024,1152]{1,0:T(8,128)} custom-call(s32[1]{0:T(128)} %bitcast.16.start, f32[8,1024,128]{2,1,0:T(8,128)} %bitcast.67, s32[8,1,512]{2,1,0:T(1,128)} %broadcast_in_dim.14.rank_ref, s32[8,1,512]{2,1,0:T(1,128)} %broadcast_xor_fusion.3.label_ref, s32[1024,1]{1,0:T(8,128)} %copy.105.own_ref, f32[512,1152]{1,0:T(8,128)} %copy-done.1), custom_call_target="tpu_custom_call" | custom-call | tf_op jit(solution)/shard_map/ladder_term/pallas_call | solution.py:249
  275.1 9.0 %ladder_term.21.refs_0_ = f32[1024,1152]{1,0:T(8,128)} custom-call(s32[1]{0:T(128)} %bitcast.15.start, f32[8,1024,128]{2,1,0:T(8,128)} %bitcast.68, s32[8,1,512]{2,1,0:T(1,128)} %broadcast_in_dim.14.rank_ref, s32[8,1,512]{2,1,0:T(1,128)} %broadcast_xor_fusion.3.label_ref, s32[1024,1]{1,0:T(8,128)} %copy.105.own_ref, ...), custom_call_target="tpu_custom_call", output_to_operand_aliasing={{}: (6, {})} | custom-call | tf_op jit(solution)/shard_map/ladder_term/pallas_call | solution.py:249
  299.4 17.5 %cycle_sums.7 = (f32[2,192,768]{2,1,0:T(8,128)}, f32[2,192,768]{2,1,0:T(8,128)}, f32[2,192,768]{2,1,0:T(8,128)}, f32[2,192,768]{2,1,0:T(8,128)}) custom-call(s32[1]{0:T(128)} %bitcast.8.base, f32[6144,1536]{1,0:T(8,128)} %ints_ref.7, s32[6144,1]{1,0:T(8,128)} %xor.135.rows_ref, s32[1,1536]{1,0:T(1,128)} %broadcast_in_dim.13.own_ref, ...), custom_call_target="tpu_custom_call" | custom-call | tf_op jit(solution)/shard_map/cycle_sums/pallas_call | solution.py:109
  316.8 9.8 %ladder_term.22.refs_0_ = f32[1024,1152]{1,0:T(8,128)} custom-call(s32[1]{0:T(128)} %bitcast.14.start, f32[8,1024,128]{2,1,0:T(8,128)} %bitcast.69, s32[8,1,512]{2,1,0:T(1,128)} %broadcast_in_dim.14.rank_ref, s32[8,1,512]{2,1,0:T(1,128)} %broadcast_xor_fusion.3.label_ref, s32[1024,1]{1,0:T(8,128)} %copy.105.own_ref, ...), custom_call_target="tpu_custom_call", output_to_operand_aliasing={{}: (6, {})} | custom-call | tf_op jit(solution)/shard_map/ladder_term/pallas_call | solution.py:249
  326.7 9.8 %ladder_term.23.refs_0_ = f32[1024,1152]{1,0:T(8,128)} custom-call(s32[1]{0:T(128)} %bitcast.13.start, f32[8,1024,128]{2,1,0:T(8,128)} %bitcast.70, s32[8,1,512]{2,1,0:T(1,128)} %broadcast_in_dim.14.rank_ref, s32[8,1,512]{2,1,0:T(1,128)} %broadcast_xor_fusion.3.label_ref, s32[1024,1]{1,0:T(8,128)} %copy.105.own_ref, ...), custom_call_target="tpu_custom_call", output_to_operand_aliasing={{}: (6, {})} | custom-call | tf_op jit(solution)/shard_map/ladder_term/pallas_call | solution.py:249
  340.7 5.2 %all-to-all-start.3 = ((f32[8,48,768]{2,1,0:T(8,128)}), f32[8,48,768]{2,1,0:T(8,128)S(1)}, u32[]{:S(2)}, u32[]{:S(2)}) async-start(f32[8,48,768]{2,1,0:T(8,128)} %owner_blocks.5), calls=%async_computation.3 | async-start | bytes 2359296 | tf_op jit(solution)/shard_map/all_to_all | solution.py:383
  353.8 9.8 %ladder_term.24.refs_0_ = f32[1024,1152]{1,0:T(8,128)} custom-call(s32[1]{0:T(128)} %bitcast.12.start, f32[8,1024,128]{2,1,0:T(8,128)} %bitcast.71, s32[8,1,512]{2,1,0:T(1,128)} %broadcast_in_dim.14.rank_ref, s32[8,1,512]{2,1,0:T(1,128)} %broadcast_xor_fusion.3.label_ref, s32[1024,1]{1,0:T(8,128)} %copy.105.own_ref, ...), custom_call_target="tpu_custom_call", output_to_operand_aliasing={{}: (6, {})} | custom-call | tf_op jit(solution)/shard_map/ladder_term/pallas_call | solution.py:249
  363.6 9.8 %ladder_term.25.refs_0_ = f32[1024,1152]{1,0:T(8,128)} custom-call(s32[1]{0:T(128)} %bitcast.11.start, f32[8,1024,128]{2,1,0:T(8,128)} %bitcast.72, s32[8,1,512]{2,1,0:T(1,128)} %broadcast_in_dim.14.rank_ref, s32[8,1,512]{2,1,0:T(1,128)} %broadcast_xor_fusion.3.label_ref, s32[1024,1]{1,0:T(8,128)} %copy.105.own_ref, ...), custom_call_target="tpu_custom_call", output_to_operand_aliasing={{}: (6, {})} | custom-call | tf_op jit(solution)/shard_map/ladder_term/pallas_call | solution.py:249
  373.5 9.8 %ladder_term.26.refs_0_ = f32[1024,1152]{1,0:T(8,128)} custom-call(s32[1]{0:T(128)} %bitcast.10.start, f32[8,1024,128]{2,1,0:T(8,128)} %bitcast.73, s32[8,1,512]{2,1,0:T(1,128)} %broadcast_in_dim.14.rank_ref, s32[8,1,512]{2,1,0:T(1,128)} %broadcast_xor_fusion.3.label_ref, s32[1024,1]{1,0:T(8,128)} %copy.105.own_ref, ...), custom_call_target="tpu_custom_call", output_to_operand_aliasing={{}: (6, {})} | custom-call | tf_op jit(solution)/shard_map/ladder_term/pallas_call | solution.py:249
  392.4 5.3 %all-to-all-start.4 = ((f32[8,48,768]{2,1,0:T(8,128)}), f32[8,48,768]{2,1,0:T(8,128)S(1)}, u32[]{:S(2)}, u32[]{:S(2)}) async-start(f32[8,48,768]{2,1,0:T(8,128)} %owner_blocks.6), calls=%async_computation.4 | async-start | bytes 2359296 | tf_op jit(solution)/shard_map/all_to_all | solution.py:383
  403.1 9.8 %ladder_term.27.ladder_ref = f32[1024,1152]{1,0:T(8,128)} custom-call(s32[1]{0:T(128)} %bitcast.start, f32[8,1024,128]{2,1,0:T(8,128)} %bitcast.74, s32[8,1,512]{2,1,0:T(1,128)} %broadcast_in_dim.14.rank_ref, s32[8,1,512]{2,1,0:T(1,128)} %broadcast_xor_fusion.3.label_ref, s32[1024,1]{1,0:T(8,128)} %copy.105.own_ref, ...), custom_call_target="tpu_custom_call", output_to_operand_aliasing={{}: (6, {})} | custom-call | tf_op jit(solution)/shard_map/ladder_term/pallas_call | solution.py:249
  418.2 8.9 %all-to-all-done.4.back_ref = f32[8,48,768]{2,1,0:T(8,128)S(1)} async-done(((f32[8,48,768]{2,1,0:T(8,128)}), f32[8,48,768]{2,1,0:T(8,128)S(1)}, u32[]{:S(2)}, u32[]{:S(2)}) %all-to-all-start.4) | async-done | bytes 1179680 | tf_op jit(solution)/shard_map/all_to_all | solution.py:383
  453.8 9.9 %all-to-all-done.5.back_ref = f32[8,48,768]{2,1,0:T(8,128)S(1)} async-done(((f32[8,48,768]{2,1,0:T(8,128)}), f32[8,48,768]{2,1,0:T(8,128)S(1)}, u32[]{:S(2)}, u32[]{:S(2)}) %all-to-all-start.5) | async-done | bytes 1179680 | tf_op jit(solution)/shard_map/all_to_all | solution.py:383
  (178 shorter events, 123.2 us)
Async XLA Ops:
  12.3 61.3 %all-to-all-start = ((f32[8,8,8,1152]{3,2,0,1:T(8,128)}), f32[8,8,8,1152]{3,2,0,1:T(8,128)}, u32[]{:S(2)}, u32[]{:S(2)}) async-start(f32[8,8,8,1152]{3,2,0,1:T(8,128)} %copy.90), calls=%async_computation | async-start | bytes 4718592 | tf_op jit(solution)/shard_map/all_to_all | solution.py:309
  18.6 54.0 %collective-permute-start = (f32[512,1152]{1,0:T(8,128)}, f32[512,1152]{1,0:T(8,128)}, u32[]{:S(2)}, u32[]{:S(2)}) collective-permute-start(f32[512,1152]{1,0:T(8,128)} %copy-done.1), channel_id=1, source_target_pairs={{0,16},{8,24},{16,0},{24,8},{1,17},{9,25},{17,1},{25,9},{2,18},{10... | collective-permute-start | bytes 7077896 | tf_op jit(solution)/shard_map/ppermute | solution.py:301
  20.1 53.5 %collective-permute-start.1 = (f32[512,1152]{1,0:T(8,128)S(1)}, f32[512,1152]{1,0:T(8,128)}, u32[]{:S(2)}, u32[]{:S(2)}) collective-permute-start(f32[512,1152]{1,0:T(8,128)S(1)} %get-tuple-element.773.amps_ref), channel_id=1, source_target_pairs={{0,8},{8,0},{16,24},{24,16},{1,9},{9,1},{17,25},{25,17},{2,10},{10... | collective-permute-start | bytes 7077896 | tf_op jit(solution)/shard_map/ppermute | solution.py:301
  75.2 59.7 %all-to-all-start.1 = ((f32[8,8,8,1152]{3,2,0,1:T(8,128)}), f32[8,8,8,1152]{3,2,0,1:T(8,128)}, u32[]{:S(2)}, u32[]{:S(2)}) async-start(f32[8,8,8,1152]{3,2,0,1:T(8,128)} %copy.92), calls=%async_computation.1 | async-start | bytes 4718592 | tf_op jit(solution)/shard_map/all_to_all | solution.py:309
  80.0 186.0 %all-gather.8.cloned.1.call-start = ((), (), s32[]{:S(2)}) async-start(), calls=%async_computation.6 | async-start | bytes 4718592 | tf_op jit(solution)/shard_map/all_gather | solution.py:342
  80.1 53.8 %collective-permute-start.3 = (f32[512,1152]{1,0:T(8,128)S(1)}, f32[512,1152]{1,0:T(8,128)}, u32[]{:S(2)}, u32[]{:S(2)}) collective-permute-start(f32[512,1152]{1,0:T(8,128)S(1)} %get-tuple-element.773.amps_ref), channel_id=1, source_target_pairs={{0,16},{8,24},{16,0},{24,8},{1,17},{9,25},{17,1},{25,9},{2,18},{10... | collective-permute-start | bytes 7077896 | tf_op jit(solution)/shard_map/ppermute | solution.py:301
  81.1 53.5 %collective-permute-start.2 = (f32[512,1152]{1,0:T(8,128)}, f32[512,1152]{1,0:T(8,128)}, u32[]{:S(2)}, u32[]{:S(2)}) collective-permute-start(f32[512,1152]{1,0:T(8,128)} %copy-done.1), channel_id=1, source_target_pairs={{0,8},{8,0},{16,24},{24,16},{1,9},{9,1},{17,25},{25,17},{2,10},{10... | collective-permute-start | bytes 7077896 | tf_op jit(solution)/shard_map/ppermute | solution.py:301
  145.3 79.6 %collective-permute-start.4 = (f32[512,1152]{1,0:T(8,128)}, f32[512,1152]{1,0:T(8,128)}, u32[]{:S(2)}, u32[]{:S(2)}) collective-permute-start(f32[512,1152]{1,0:T(8,128)} %collective-permute-done.amps_ref), channel_id=1, source_target_pairs={{0,8},{8,0},{16,24},{24,16},{1,9},{9,1},{17,25},{25,17},{2,10},{10... | collective-permute-start | bytes 7077896 | tf_op jit(solution)/shard_map/ppermute | solution.py:301
  146.9 78.0 %collective-permute-start.5 = (f32[512,1152]{1,0:T(8,128)}, f32[512,1152]{1,0:T(8,128)}, u32[]{:S(2)}, u32[]{:S(2)}) collective-permute-start(f32[512,1152]{1,0:T(8,128)} %collective-permute-done.1.amps_ref), channel_id=1, source_target_pairs={{0,16},{8,24},{16,0},{24,8},{1,17},{9,25},{17,1},{25,9},{2,18},{10... | collective-permute-start | bytes 7077896 | tf_op jit(solution)/shard_map/ppermute | solution.py:301
  171.3 53.6 %collective-permute-start.6 = (f32[2,192,768]{2,1,0:T(8,128)}, f32[2,192,768]{2,1,0:T(8,128)S(1)}, u32[]{:S(2)}, u32[]{:S(2)}) collective-permute-start(f32[2,192,768]{2,1,0:T(8,128)} %get-tuple-element.793), channel_id=1, source_target_pairs={{0,16},{8,24},{16,0},{24,8},{1,17},{9,25},{17,1},{25,9},{2,18},{10... | collective-permute-start | bytes 3538952 | tf_op jit(solution)/shard_map/ppermute | solution.py:301
  172.5 52.4 %collective-permute-start.7 = (f32[2,192,768]{2,1,0:T(8,128)}, f32[2,192,768]{2,1,0:T(8,128)S(1)}, u32[]{:S(2)}, u32[]{:S(2)}) collective-permute-start(f32[2,192,768]{2,1,0:T(8,128)} %get-tuple-element.794), channel_id=1, source_target_pairs={{0,8},{8,0},{16,24},{24,16},{1,9},{9,1},{17,25},{25,17},{2,10},{10... | collective-permute-start | bytes 3538952 | tf_op jit(solution)/shard_map/ppermute | solution.py:301
  224.9 59.3 %collective-permute-start.10 = (f32[2,192,768]{2,1,0:T(8,128)}, f32[2,192,768]{2,1,0:T(8,128)S(1)}, u32[]{:S(2)}, u32[]{:S(2)}) collective-permute-start(f32[2,192,768]{2,1,0:T(8,128)} %get-tuple-element.816), channel_id=1, source_target_pairs={{0,16},{8,24},{16,0},{24,8},{1,17},{9,25},{17,1},{25,9},{2,18},{10... | collective-permute-start | bytes 3538952 | tf_op jit(solution)/shard_map/ppermute | solution.py:301
  225.8 58.4 %collective-permute-start.11 = (f32[2,192,768]{2,1,0:T(8,128)}, f32[2,192,768]{2,1,0:T(8,128)}, u32[]{:S(2)}, u32[]{:S(2)}) collective-permute-start(f32[2,192,768]{2,1,0:T(8,128)} %get-tuple-element.817), channel_id=1, source_target_pairs={{0,8},{8,0},{16,24},{24,16},{1,9},{9,1},{17,25},{25,17},{2,10},{10... | collective-permute-start | bytes 3538952 | tf_op jit(solution)/shard_map/ppermute | solution.py:301
  227.2 56.9 %collective-permute-start.9 = (f32[1,192,768]{2,1,0:T(8,128)}, f32[1,192,768]{2,1,0:T(8,128)}, u32[]{:S(2)}, u32[]{:S(2)}) collective-permute-start(f32[1,192,768]{2,1,0:T(8,128)} %slice_add_fusion.6), channel_id=1, source_target_pairs={{0,16},{8,24},{16,0},{24,8},{1,17},{9,25},{17,1},{25,9},{2,18},{10... | collective-permute-start | bytes 1769480 | tf_op jit(solution)/shard_map/ppermute | solution.py:301
  229.3 54.8 %collective-permute-start.8 = (f32[1,192,768]{2,1,0:T(8,128)}, f32[1,192,768]{2,1,0:T(8,128)}, u32[]{:S(2)}, u32[]{:S(2)}) collective-permute-start(f32[1,192,768]{2,1,0:T(8,128)} %slice_add_fusion.7), channel_id=1, source_target_pairs={{0,8},{8,0},{16,24},{24,16},{1,9},{9,1},{17,25},{25,17},{2,10},{10... | collective-permute-start | bytes 1769480 | tf_op jit(solution)/shard_map/ppermute | solution.py:301
  288.4 48.1 %all-to-all-start.2 = ((f32[8,48,768]{2,1,0:T(8,128)}), f32[8,48,768]{2,1,0:T(8,128)S(1)}, u32[]{:S(2)}, u32[]{:S(2)}) async-start(f32[8,48,768]{2,1,0:T(8,128)} %owner_blocks.4), calls=%async_computation.2 | async-start | bytes 2359296 | tf_op jit(solution)/shard_map/all_to_all | solution.py:383
  292.4 44.1 %collective-permute-start.14 = (f32[2,192,768]{2,1,0:T(8,128)}, f32[2,192,768]{2,1,0:T(8,128)}, u32[]{:S(2)}, u32[]{:S(2)}) collective-permute-start(f32[2,192,768]{2,1,0:T(8,128)} %get-tuple-element.842), channel_id=1, source_target_pairs={{0,16},{8,24},{16,0},{24,8},{1,17},{9,25},{17,1},{25,9},{2,18},{10... | collective-permute-start | bytes 3538952 | tf_op jit(solution)/shard_map/ppermute | solution.py:301
  293.7 42.9 %collective-permute-start.15 = (f32[2,192,768]{2,1,0:T(8,128)}, f32[2,192,768]{2,1,0:T(8,128)}, u32[]{:S(2)}, u32[]{:S(2)}) collective-permute-start(f32[2,192,768]{2,1,0:T(8,128)} %get-tuple-element.843), channel_id=1, source_target_pairs={{0,8},{8,0},{16,24},{24,16},{1,9},{9,1},{17,25},{25,17},{2,10},{10... | collective-permute-start | bytes 3538952 | tf_op jit(solution)/shard_map/ppermute | solution.py:301
  296.1 40.4 %collective-permute-start.13 = (f32[1,192,768]{2,1,0:T(8,128)}, f32[1,192,768]{2,1,0:T(8,128)S(1)}, u32[]{:S(2)}, u32[]{:S(2)}) collective-permute-start(f32[1,192,768]{2,1,0:T(8,128)} %slice_add_fusion.4), channel_id=1, source_target_pairs={{0,16},{8,24},{16,0},{24,8},{1,17},{9,25},{17,1},{25,9},{2,18},{10... | collective-permute-start | bytes 1769480 | tf_op jit(solution)/shard_map/ppermute | solution.py:301
  297.9 38.6 %collective-permute-start.12 = (f32[1,192,768]{2,1,0:T(8,128)}, f32[1,192,768]{2,1,0:T(8,128)S(1)}, u32[]{:S(2)}, u32[]{:S(2)}) collective-permute-start(f32[1,192,768]{2,1,0:T(8,128)} %slice_add_fusion.5), channel_id=1, source_target_pairs={{0,8},{8,0},{16,24},{24,16},{1,9},{9,1},{17,25},{25,17},{2,10},{10... | collective-permute-start | bytes 1769480 | tf_op jit(solution)/shard_map/ppermute | solution.py:301
  340.7 47.3 %all-to-all-start.3 = ((f32[8,48,768]{2,1,0:T(8,128)}), f32[8,48,768]{2,1,0:T(8,128)S(1)}, u32[]{:S(2)}, u32[]{:S(2)}) async-start(f32[8,48,768]{2,1,0:T(8,128)} %owner_blocks.5), calls=%async_computation.3 | async-start | bytes 2359296 | tf_op jit(solution)/shard_map/all_to_all | solution.py:383
  345.9 42.1 %collective-permute-start.18 = (f32[2,192,768]{2,1,0:T(8,128)}, f32[2,192,768]{2,1,0:T(8,128)}, u32[]{:S(2)}, u32[]{:S(2)}) collective-permute-start(f32[2,192,768]{2,1,0:T(8,128)} %get-tuple-element.861), channel_id=1, source_target_pairs={{0,16},{8,24},{16,0},{24,8},{1,17},{9,25},{17,1},{25,9},{2,18},{10... | collective-permute-start | bytes 3538952 | tf_op jit(solution)/shard_map/ppermute | solution.py:301
  347.1 41.0 %collective-permute-start.19 = (f32[2,192,768]{2,1,0:T(8,128)}, f32[2,192,768]{2,1,0:T(8,128)}, u32[]{:S(2)}, u32[]{:S(2)}) collective-permute-start(f32[2,192,768]{2,1,0:T(8,128)} %get-tuple-element.862), channel_id=1, source_target_pairs={{0,8},{8,0},{16,24},{24,16},{1,9},{9,1},{17,25},{25,17},{2,10},{10... | collective-permute-start | bytes 3538952 | tf_op jit(solution)/shard_map/ppermute | solution.py:301
  349.5 37.6 %collective-permute-start.17 = (f32[1,192,768]{2,1,0:T(8,128)}, f32[1,192,768]{2,1,0:T(8,128)S(1)}, u32[]{:S(2)}, u32[]{:S(2)}) collective-permute-start(f32[1,192,768]{2,1,0:T(8,128)} %slice_add_fusion.2), channel_id=1, source_target_pairs={{0,16},{8,24},{16,0},{24,8},{1,17},{9,25},{17,1},{25,9},{2,18},{10... | collective-permute-start | bytes 1769480 | tf_op jit(solution)/shard_map/ppermute | solution.py:301
  (41 other events, 660.9 us)
Sparse Core Ops, SparseCore 0:
  145.4 47.6 all-gather.7

commit v2 on v1

--- a/solution.py
+++ b/solution.py
@@ -27,11 +27,11 @@
     return jnp.dot(left, right, preferred_element_type=jnp.float32)
 
 
-def to_cycle_kernel(occ, depth, moved_ref, high_ref, low_ref, cells, rows):
-    _, height, width = moved_ref.shape
-    sources, count = height // depth, width // occ
+def to_cycle_kernel(occ, moved_ref, high_ref, low_ref, cells, rows):
+    sources, _, depth, width = moved_ref.shape
+    count = width // occ
     for source in range(sources):
-        value = moved_ref[0, source * depth : (source + 1) * depth, :]
+        value = moved_ref[source, 0]
         for k in range(count):
             at = (source * count + k) * 8
             cells[at : at + depth, 0:occ] = value[:, k * occ : (k + 1) * occ]
@@ -44,13 +44,13 @@
 
 
 def to_cycle_rows(moved, occ):
-    count, sources, depth, width = moved.shape
+    sources, count, depth, width = moved.shape
     height = sources * width // occ
     shape = jax.ShapeDtypeStruct((count * height, depth * occ), jnp.bfloat16)
     return pl.pallas_call(
-        functools.partial(to_cycle_kernel, occ, depth),
+        functools.partial(to_cycle_kernel, occ),
         grid=(count,),
-        in_specs=[pl.BlockSpec((1, sources * depth, width), lambda c: (c, 0, 0))],
+        in_specs=[pl.BlockSpec((sources, 1, depth, width), lambda c: (0, c, 0, 0))],
         out_specs=[pl.BlockSpec((height, depth * occ), lambda c: (c, 0))] * 2,
         out_shape=[shape, shape],
         scratch_shapes=[
@@ -60,7 +60,7 @@
         compiler_params=PARAMS,
         cost_estimate=SMALL,
         name="to_cycle_rows",
-    )(moved.reshape(count, sources * depth, width))
+    )(moved)
 
 
 def cycle_kernel(
@@ -190,7 +190,7 @@
             in_specs=[
                 pl.BlockSpec(back.shape, lambda step, at: (0, 0, 0)),
                 block,
-                pl.BlockSpec((height, 1), lambda step, at: (0, 0)),
+                pl.BlockSpec((height, 1), lambda step, at: (at[0], 0)),
                 pl.BlockSpec((1, columns), lambda step, at: (0, 0)),
             ],
             out_specs=block,
@@ -208,7 +208,7 @@
         jnp.full((1,), part, jnp.int32),
         back,
         ladder,
-        row_energy[part * height : (part + 1) * height],
+        row_energy,
         col_energy,
     )
 
@@ -305,12 +305,29 @@
     first, second = amps[:half_rows], amps[half_rows:]
 
     def to_cycle(value):
-        blocks = value.reshape(half_virt, col_count, virt_cols, columns)
-        return lax.all_to_all(blocks, "col", split_axis=1, concat_axis=1, tiled=True)
+        blocks = value.reshape(half_virt, col_count, virt_cols, columns).transpose(1, 0, 2, 3)
+        return lax.all_to_all(blocks, "col", split_axis=0, concat_axis=0, tiled=True)
 
     first_2, second_1 = swap(first, 2), swap(second, 1)
     moved = to_cycle(first)
-    held_first, held, first_2, second_1, moved = barrier((first, second, first_2, second_1, moved))
+
+    blocks = virt_pairs.reshape(col_count, ladder_cols)
+    place = jnp.arange(ladder_cols)
+    same = (blocks[:, :, None] == blocks[:, None, :]) & (place[None, None, :] < place[None, :, None])
+    rank = jnp.sum(same, axis=2, dtype=jnp.int32)
+    turns = jnp.max(rank) // WINDOW + 1
+
+    own_virt = lax.dynamic_slice_in_dim(virt_energy, row_index * virt_local, virt_local)
+    own_occ = lax.dynamic_slice_in_dim(occ_energy, col_index * occ_local, occ_local)
+    row_energy = (own_virt[:, None] + virt_energy[None, :]).reshape(-1)[:, None]
+    col_energy = (own_occ[:, None] + occ_energy[None, :]).reshape(-1)[None, :]
+
+    mixed_rows, mixed_cols = mixed_pairs[:, None], own_mixed[None, :]
+    small = (mixed_rows, mixed_cols, row_energy, col_energy, rank, turns)
+    held_first, held, first_2, second_1, moved, small = barrier(
+        (first, second, first_2, second_1, moved, small)
+    )
+    mixed_rows, mixed_cols, row_energy, col_energy, rank, turns = small
     first_1, second_2 = swap(held_first, 1), swap(held, 2)
     rights = to_cycle_rows(moved, occ_total)
     moved = to_cycle(held)
@@ -320,11 +337,6 @@
     first_3, second_3 = swap(first_2, 1), swap(second_1, 2)
     rights = rights + to_cycle_rows(moved, occ_total)
 
-    blocks = virt_pairs.reshape(col_count, ladder_cols)
-    place = jnp.arange(ladder_cols)
-    same = (blocks[:, :, None] == blocks[:, None, :]) & (place[None, None, :] < place[None, :, None])
-    rank = jnp.sum(same, axis=2, dtype=jnp.int32)
-    turns = jnp.max(rank) // WINDOW + 1
     own_rank = lax.dynamic_index_in_dim(rank, col_index, 0, keepdims=False)
     own_block = lax.dynamic_index_in_dim(blocks, col_index, 0, keepdims=False)
     masked_ints = jnp.where(own_pairs[:, None] == own_block[None, :], ladder_ints, jnp.float32(0.0))
@@ -359,14 +371,9 @@
     packed, rights = barrier((packed_ints(0), rights))
     packed = gathered(packed)
 
-    own_virt = lax.dynamic_slice_in_dim(virt_energy, row_index * virt_local, virt_local)
-    own_occ = lax.dynamic_slice_in_dim(occ_energy, col_index * occ_local, occ_local)
-    row_energy = (own_virt[:, None] + virt_energy[None, :]).reshape(-1)[:, None]
-    col_energy = (own_occ[:, None] + occ_energy[None, :]).reshape(-1)[None, :]
-
     sums = functools.partial(
-        cycle_sums, row_index=row_index, ints=cycle_ints, labels=mixed_pairs[:, None],
-        own_labels=own_mixed[None, :],
+        cycle_sums, row_index=row_index, ints=cycle_ints, labels=mixed_rows,
+        own_labels=mixed_cols,
     )
     def pass_on(keep, near):
         return swap(keep[0][1:] + near[0][1:], 1), swap(keep[1][1:] + near[1][1:], 2)
@@ -392,41 +399,44 @@
     near_0 = send(out_0)
     rights, keep_0 = barrier((rights, keep_0))
     out_1, keep_1 = part_sums(1, rights)
-
-    rights, first_3, second_3, near_0, keep_0, out_1, keep_1 = barrier(
-        (rights, first_3, second_3, near_0, keep_0, out_1, keep_1)
+    rights, keep_1 = barrier((rights, keep_1))
+    out_2, keep_2 = part_sums(2, rights)
+    packed, keep_2 = barrier((packed, keep_2))
+    ladder = ladder_from(packed, 0, pieces[:1])
+
+    rights, ladder, first_3, second_3, near_0, keep_0, out_1, keep_1, out_2, keep_2 = barrier(
+        (rights, ladder, first_3, second_3, near_0, keep_0, out_1, keep_1, out_2, keep_2)
     )
     pieces += [(3, 0, first_3), (3, 1, second_3)]
     far_0, near_1 = pass_on(keep_0, near_0), send(out_1)
-    out_2, keep_2 = part_sums(2, rights)
-    packed, keep_2 = barrier((packed, keep_2))
-    ladder = ladder_from(packed, 0, pieces[:2])
-
-    rights, ladder, far_0, near_0, keep_0, near_1, keep_1, out_2, keep_2 = barrier(
-        (rights, ladder, far_0, near_0, keep_0, near_1, keep_1, out_2, keep_2)
+    ladder = ladder_from(packed, 0, pieces[1:3], ladder)
+    ladder, far_0 = barrier((ladder, far_0))
+    blocks_0 = owned(keep_0, near_0, far_0)
+
+    rights, ladder, _, near_1, keep_1, out_2, keep_2 = barrier(
+        (rights, ladder, blocks_0, near_1, keep_1, out_2, keep_2)
     )
     far_1, near_2 = pass_on(keep_1, near_1), send(out_2)
-    back_0 = to_owner(owned(keep_0, near_0, far_0))
     out_3, keep_3 = part_sums(3, rights)
-    ladder, keep_3 = barrier((ladder, keep_3))
-    ladder = ladder_from(packed, 0, pieces[2:4], ladder)
-
-    ladder, back_0, far_1, near_1, keep_1, near_2, keep_2, out_3, keep_3 = barrier(
-        (ladder, back_0, far_1, near_1, keep_1, near_2, keep_2, out_3, keep_3)
-    )
+    keep_3, far_1 = barrier((keep_3, far_1))
+    blocks_1 = owned(keep_1, near_1, far_1)
+    _, ladder = barrier((blocks_1, ladder))
+    ladder = ladder_from(packed, 0, pieces[3:4], ladder)
+
+    ladder, near_2, keep_2, out_3, keep_3 = barrier((ladder, near_2, keep_2, out_3, keep_3))
     far_2, near_3 = pass_on(keep_2, near_2), send(out_3)
-    back_1 = to_owner(owned(keep_1, near_1, far_1))
-    ladder = ladder_from(packed, 0, pieces[4:7], ladder)
-
-    ladder, back_1, far_2, near_2, keep_2, near_3, keep_3 = barrier(
-        (ladder, back_1, far_2, near_2, keep_2, near_3, keep_3)
-    )
+    ladder = ladder_from(packed, 0, pieces[4:6], ladder)
+    ladder, far_2 = barrier((ladder, far_2))
+    blocks_2 = owned(keep_2, near_2, far_2)
+
+    ladder, _, near_3, keep_3 = barrier((ladder, blocks_2, near_3, keep_3))
     far_3 = pass_on(keep_3, near_3)
-    back_2 = to_owner(owned(keep_2, near_2, far_2))
+    ladder = ladder_from(packed, 0, pieces[6:7], ladder)
+    ladder, far_3 = barrier((ladder, far_3))
+    blocks_3 = owned(keep_3, near_3, far_3)
+    back_0, back_1, back_2, back_3 = map(to_owner, (blocks_0, blocks_1, blocks_2, blocks_3))
+    _, ladder = barrier((blocks_3, ladder))
     ladder = ladder_from(packed, 0, pieces[7:], ladder)
-
-    ladder, back_2, far_3, near_3, keep_3 = barrier((ladder, back_2, far_3, near_3, keep_3))
-    back_3 = to_owner(owned(keep_3, near_3, far_3))
     backs = [back_0, back_1, back_2, back_3]
     update = ladder
     for part in range(PARTS):

time: 482 us -> 427 us (0.89)
  waiting for transfers between devices: 149 us -> 119 us
  Pallas kernels: 205 us -> 192 us
  local copies, waits for them, and re-layouts: 33.2 us -> 20.4 us
    ppermute x22, waiting for transfers between devices: 129 us -> 113 us  [swap(): return lax.ppermute(value, 'row', [(i, i ^ flip) for i in range(row_count)])]
    pallas_call x4, Pallas kernels: 83.1 us -> 70.2 us  [cycle_sums(): pl.pallas_call(cycle_kernel, grid_spec=pltpu.PrefetchScalarGridSpec(num_s...]
    all_to_all x4, waiting for transfers between devices: 18.9 us -> 6.06 us  [to_owner(): lax.all_to_all(blocks, 'col', split_axis=0, concat_axis=0, tiled=True)]
    xor x9, local copies, waits for them, and re-layouts: 6.67 us -> 0.65 us  [pair_labels(): return jnp.bitwise_xor(first[:, None], second[None, :]).reshape(-1)]
  transfers between devices with their start and end apart: 29 -> 29, of which waited for: 12 -> 10; matrix products, arithmetic and copies ran while one was open for 8% -> 6% of each run, Pallas kernels for 38% -> 43%
where the time goes in v2:
time: 427 us; the launch traced here: 422 us
  Pallas kernels  192 us (45%)
  waiting for transfers between devices  119 us (28%)
  starting transfers between devices  53.9 us (13%)
  local copies, waits for them, and re-layouts  20.4 us (5%)
  other arithmetic  19 us (4%)
  between operations  16.5 us (4%)
    ppermute x22, waiting for transfers between devices, swap(): return lax.ppermute(value, 'row', [(i, i ^ flip) for i in range(row_count)])  113 us
    pallas_call x8, Pallas kernels, ladder_term(): pl.pallas_call(functools.partial(ladder_kernel, fresh), grid_spec=pltpu.P...  77.5 us
    pallas_call x4, Pallas kernels, cycle_sums(): pl.pallas_call(cycle_kernel, grid_spec=pltpu.PrefetchScalarGridSpec(num_s...  70.2 us
    ppermute x22, starting transfers between devices, swap(): return lax.ppermute(value, 'row', [(i, i ^ flip) for i in range(row_count)])  23.6 us
    all_to_all x4, starting transfers between devices, to_owner(): lax.all_to_all(blocks, 'col', split_axis=0, concat_axis=0, tiled=True)  18.6 us
    pallas_call x4, Pallas kernels, with_cycle(): pl.pallas_call(functools.partial(update_kernel, occ, occ_local), grid_spe...  16.5 us
    pallas_call x2, Pallas kernels, to_cycle_rows(): pl.pallas_call(functools.partial(to_cycle_kernel, occ), grid=(count,), in...  14.6 us
    pallas_call x4, Pallas kernels, owner_blocks(): pl.pallas_call(functools.partial(owner_kernel, occ_local), grid=(1,), in_...  12.7 us
  transfers between devices with their start and end apart: 29, of which 10 were waited for; matrix products, arithmetic and copies ran while one was open for 6% of the time, Pallas kernels for 43%

profile of v2, /device:TPU:0, one launch (start us, length us, event | category | flops | bytes accessed | tf_op | source)
XLA Modules:
  0.0 421.9 jit_solution(5091790659717437061)
XLA Ops:
  11.4 6.5 %all-to-all-start = ((f32[8,8,8,1152]{3,2,1,0:T(8,128)}), f32[8,8,8,1152]{3,2,1,0:T(8,128)}, u32[]{:S(2)}, u32[]{:S(2)}) async-start(f32[8,8,8,1152]{3,2,1,0:T(8,128)} %bitcast.82), calls=%async_computation | async-start | bytes 4718592 | tf_op jit(solution)/shard_map/all_to_all | solution.py:309
  29.4 42.5 %collective-permute-done.amps_ref = f32[512,1152]{1,0:T(8,128)} collective-permute-done((f32[512,1152]{1,0:T(8,128)}, f32[512,1152]{1,0:T(8,128)}, u32[]{:S(2)}, u32[]{:S(2)}) %collective-permute-start) | collective-permute-done | bytes 2359328 | tf_op jit(solution)/shard_map/ppermute | solution.py:301
  74.5 4.7 %all-to-all-start.1 = ((f32[8,8,8,1152]{3,2,1,0:T(8,128)}), f32[8,8,8,1152]{3,2,1,0:T(8,128)}, u32[]{:S(2)}, u32[]{:S(2)}) async-start(f32[8,8,8,1152]{3,2,1,0:T(8,128)} %bitcast.83), calls=%async_computation.1 | async-start | bytes 4718592 | tf_op jit(solution)/shard_map/all_to_all | solution.py:309
  84.2 7.4 %to_cycle_rows.2 = (bf16[768,768]{1,0:T(8,128)(2,1)}, bf16[768,768]{1,0:T(8,128)(2,1)}) custom-call(f32[8,8,8,1152]{3,2,1,0:T(8,128)} %all-to-all-done.moved_ref), custom_call_target="tpu_custom_call" | custom-call | tf_op jit(solution)/shard_map/to_cycle_rows/pallas_call | solution.py:50
  93.3 40.4 %collective-permute-done.2.amps_ref = f32[512,1152]{1,0:T(8,128)} collective-permute-done((f32[512,1152]{1,0:T(8,128)}, f32[512,1152]{1,0:T(8,128)}, u32[]{:S(2)}, u32[]{:S(2)}) %collective-permute-start.2) | collective-permute-done | bytes 2359328 | tf_op jit(solution)/shard_map/ppermute | solution.py:301
  134.7 7.2 %to_cycle_rows.3 = (bf16[768,768]{1,0:T(8,128)(2,1)}, bf16[768,768]{1,0:T(8,128)(2,1)}) custom-call(f32[8,8,8,1152]{3,2,1,0:T(8,128)} %all-to-all-done.1.moved_ref), custom_call_target="tpu_custom_call" | custom-call | tf_op jit(solution)/shard_map/to_cycle_rows/pallas_call | solution.py:50
  145.8 17.7 %cycle_sums.4 = (f32[2,192,768]{2,1,0:T(8,128)}, f32[2,192,768]{2,1,0:T(8,128)}, f32[2,192,768]{2,1,0:T(8,128)}, f32[2,192,768]{2,1,0:T(8,128)}) custom-call(s32[1]{0:T(128)} %bitcast.8.base, f32[6144,1536]{1,0:T(8,128)} %ints_ref.7, s32[6144,1]{1,0:T(8,128)} %copy.70.rows_ref, s32[1,1536]{1,0:T(1,128)} %broadcast_in_dim.12.own_ref, ...), custom_call_target="tpu_custom_call" | custom-call | tf_op jit(solution)/shard_map/cycle_sums/pallas_call | solution.py:109
  168.1 17.5 %cycle_sums.5 = (f32[2,192,768]{2,1,0:T(8,128)}, f32[2,192,768]{2,1,0:T(8,128)}, f32[2,192,768]{2,1,0:T(8,128)}, f32[2,192,768]{2,1,0:T(8,128)}) custom-call(s32[1]{0:T(128)} %bitcast.8.base, f32[6144,1536]{1,0:T(8,128)} %ints_ref.7, s32[6144,1]{1,0:T(8,128)} %copy.70.rows_ref, s32[1,1536]{1,0:T(1,128)} %broadcast_in_dim.12.own_ref, ...), custom_call_target="tpu_custom_call" | custom-call | tf_op jit(solution)/shard_map/cycle_sums/pallas_call | solution.py:109
  185.7 17.5 %cycle_sums.6 = (f32[2,192,768]{2,1,0:T(8,128)}, f32[2,192,768]{2,1,0:T(8,128)}, f32[2,192,768]{2,1,0:T(8,128)}, f32[2,192,768]{2,1,0:T(8,128)}) custom-call(s32[1]{0:T(128)} %bitcast.8.base, f32[6144,1536]{1,0:T(8,128)} %ints_ref.7, s32[6144,1]{1,0:T(8,128)} %copy.70.rows_ref, s32[1,1536]{1,0:T(1,128)} %broadcast_in_dim.12.own_ref, ...), custom_call_target="tpu_custom_call" | custom-call | tf_op jit(solution)/shard_map/cycle_sums/pallas_call | solution.py:109
  203.2 9.4 %ladder_term.20.refs_0_ = f32[1024,1152]{1,0:T(8,128)} custom-call(s32[1]{0:T(128)} %bitcast.12.start, f32[8,1024,128]{2,1,0:T(8,128)} %bitcast.72, s32[8,1,512]{2,1,0:T(1,128)} %broadcast_in_dim.13.rank_ref, s32[8,1,512]{2,1,0:T(1,128)} %broadcast_xor_fusion.3.label_ref, s32[1024,1]{1,0:T(8,128)} %copy.77.own_ref, f32[512,1152]{1,0:T(8,128)} %copy-done.2), custom_call_target="tpu_custom_call" | custom-call | tf_op jit(solution)/shard_map/ladder_term/pallas_call | solution.py:249
  212.6 8.3 %collective-permute-done.6.refs_1_ = f32[2,192,768]{2,1,0:T(8,128)} collective-permute-done((f32[2,192,768]{2,1,0:T(8,128)}, f32[2,192,768]{2,1,0:T(8,128)}, u32[]{:S(2)}, u32[]{:S(2)}) %collective-permute-start.6) | collective-permute-done | bytes 1179680 | tf_op jit(solution)/shard_map/ppermute | solution.py:301
  228.9 9.0 %ladder_term.21.refs_0_ = f32[1024,1152]{1,0:T(8,128)} custom-call(s32[1]{0:T(128)} %bitcast.14.start, f32[8,1024,128]{2,1,0:T(8,128)} %bitcast.73, s32[8,1,512]{2,1,0:T(1,128)} %broadcast_in_dim.13.rank_ref, s32[8,1,512]{2,1,0:T(1,128)} %broadcast_xor_fusion.3.label_ref, s32[1024,1]{1,0:T(8,128)} %copy.77.own_ref, ...), custom_call_target="tpu_custom_call", output_to_operand_aliasing={{}: (6, {})} | custom-call | tf_op jit(solution)/shard_map/ladder_term/pallas_call | solution.py:249
  237.9 9.8 %ladder_term.22.refs_0_ = f32[1024,1152]{1,0:T(8,128)} custom-call(s32[1]{0:T(128)} %bitcast.13.start, f32[8,1024,128]{2,1,0:T(8,128)} %bitcast.74, s32[8,1,512]{2,1,0:T(1,128)} %broadcast_in_dim.13.rank_ref, s32[8,1,512]{2,1,0:T(1,128)} %broadcast_xor_fusion.3.label_ref, s32[1024,1]{1,0:T(8,128)} %copy.77.own_ref, ...), custom_call_target="tpu_custom_call", output_to_operand_aliasing={{}: (6, {})} | custom-call | tf_op jit(solution)/shard_map/ladder_term/pallas_call | solution.py:249
  256.8 7.7 %collective-permute-done.10.refs_1_ = f32[2,192,768]{2,1,0:T(8,128)} collective-permute-done((f32[2,192,768]{2,1,0:T(8,128)}, f32[2,192,768]{2,1,0:T(8,128)}, u32[]{:S(2)}, u32[]{:S(2)}) %collective-permute-start.10) | collective-permute-done | bytes 1179680 | tf_op jit(solution)/shard_map/ppermute | solution.py:301
  271.0 17.4 %cycle_sums.7 = (f32[2,192,768]{2,1,0:T(8,128)}, f32[2,192,768]{2,1,0:T(8,128)}, f32[2,192,768]{2,1,0:T(8,128)}, f32[2,192,768]{2,1,0:T(8,128)}) custom-call(s32[1]{0:T(128)} %bitcast.8.base, f32[6144,1536]{1,0:T(8,128)} %ints_ref.7, s32[6144,1]{1,0:T(8,128)} %copy.70.rows_ref, s32[1,1536]{1,0:T(1,128)} %broadcast_in_dim.12.own_ref, ...), custom_call_target="tpu_custom_call" | custom-call | tf_op jit(solution)/shard_map/cycle_sums/pallas_call | solution.py:109
  297.1 9.9 %ladder_term.23.refs_0_ = f32[1024,1152]{1,0:T(8,128)} custom-call(s32[1]{0:T(128)} %bitcast.11.start, f32[8,1024,128]{2,1,0:T(8,128)} %bitcast.75, s32[8,1,512]{2,1,0:T(1,128)} %broadcast_in_dim.13.rank_ref, s32[8,1,512]{2,1,0:T(1,128)} %broadcast_xor_fusion.3.label_ref, s32[1024,1]{1,0:T(8,128)} %copy.77.own_ref, ...), custom_call_target="tpu_custom_call", output_to_operand_aliasing={{}: (6, {})} | custom-call | tf_op jit(solution)/shard_map/ladder_term/pallas_call | solution.py:249
  314.3 9.8 %ladder_term.24.refs_0_ = f32[1024,1152]{1,0:T(8,128)} custom-call(s32[1]{0:T(128)} %bitcast.10.start, f32[8,1024,128]{2,1,0:T(8,128)} %bitcast.76, s32[8,1,512]{2,1,0:T(1,128)} %broadcast_in_dim.13.rank_ref, s32[8,1,512]{2,1,0:T(1,128)} %broadcast_xor_fusion.3.label_ref, s32[1024,1]{1,0:T(8,128)} %copy.77.own_ref, ...), custom_call_target="tpu_custom_call", output_to_operand_aliasing={{}: (6, {})} | custom-call | tf_op jit(solution)/shard_map/ladder_term/pallas_call | solution.py:249
  324.2 9.8 %ladder_term.25.refs_0_ = f32[1024,1152]{1,0:T(8,128)} custom-call(s32[1]{0:T(128)} %bitcast.start, f32[8,1024,128]{2,1,0:T(8,128)} %bitcast.77, s32[8,1,512]{2,1,0:T(1,128)} %broadcast_in_dim.13.rank_ref, s32[8,1,512]{2,1,0:T(1,128)} %broadcast_xor_fusion.3.label_ref, s32[1024,1]{1,0:T(8,128)} %copy.77.own_ref, ...), custom_call_target="tpu_custom_call", output_to_operand_aliasing={{}: (6, {})} | custom-call | tf_op jit(solution)/shard_map/ladder_term/pallas_call | solution.py:249
  338.9 5.2 %all-to-all-start.3 = ((f32[8,48,768]{2,1,0:T(8,128)}), f32[8,48,768]{2,1,0:T(8,128)S(1)}, u32[]{:S(2)}, u32[]{:S(2)}) async-start(f32[8,48,768]{2,1,0:T(8,128)} %owner_blocks.6), calls=%async_computation.3 | async-start | bytes 2359296 | tf_op jit(solution)/shard_map/all_to_all | solution.py:390
  344.1 8.1 %collective-permute-done.18.refs_1_ = f32[2,192,768]{2,1,0:T(8,128)} collective-permute-done((f32[2,192,768]{2,1,0:T(8,128)}, f32[2,192,768]{2,1,0:T(8,128)}, u32[]{:S(2)}, u32[]{:S(2)}) %collective-permute-start.18) | collective-permute-done | bytes 1179680 | tf_op jit(solution)/shard_map/ppermute | solution.py:301
  358.0 9.8 %ladder_term.26.refs_0_ = f32[1024,1152]{1,0:T(8,128)} custom-call(s32[1]{0:T(128)} %bitcast.15.start, f32[8,1024,128]{2,1,0:T(8,128)} %bitcast.78, s32[8,1,512]{2,1,0:T(1,128)} %broadcast_in_dim.13.rank_ref, s32[8,1,512]{2,1,0:T(1,128)} %broadcast_xor_fusion.3.label_ref, s32[1024,1]{1,0:T(8,128)} %copy.77.own_ref, ...), custom_call_target="tpu_custom_call", output_to_operand_aliasing={{}: (6, {})} | custom-call | tf_op jit(solution)/shard_map/ladder_term/pallas_call | solution.py:249
  375.8 4.6 %all-to-all-start.2 = ((f32[8,48,768]{2,1,0:T(8,128)}), f32[8,48,768]{2,1,0:T(8,128)S(1)}, u32[]{:S(2)}, u32[]{:S(2)}) async-start(f32[8,48,768]{2,1,0:T(8,128)} %owner_blocks.7), calls=%async_computation.2 | async-start | bytes 2359296 | tf_op jit(solution)/shard_map/all_to_all | solution.py:390
  381.4 9.9 %ladder_term.27.ladder_ref = f32[1024,1152]{1,0:T(8,128)} custom-call(s32[1]{0:T(128)} %bitcast.16.start, f32[8,1024,128]{2,1,0:T(8,128)} %bitcast.79, s32[8,1,512]{2,1,0:T(1,128)} %broadcast_in_dim.13.rank_ref, s32[8,1,512]{2,1,0:T(1,128)} %broadcast_xor_fusion.3.label_ref, s32[1024,1]{1,0:T(8,128)} %copy.77.own_ref, ...), custom_call_target="tpu_custom_call", output_to_operand_aliasing={{}: (6, {})} | custom-call | tf_op jit(solution)/shard_map/ladder_term/pallas_call | solution.py:249
  403.7 6.0 %all-to-all-done.2.back_ref = f32[8,48,768]{2,1,0:T(8,128)S(1)} async-done(((f32[8,48,768]{2,1,0:T(8,128)}), f32[8,48,768]{2,1,0:T(8,128)S(1)}, u32[]{:S(2)}, u32[]{:S(2)}) %all-to-all-start.2) | async-done | bytes 1179680 | tf_op jit(solution)/shard_map/all_to_all | solution.py:390
  (166 shorter events, 109.1 us)
Async XLA Ops:
  11.4 61.5 %all-to-all-start = ((f32[8,8,8,1152]{3,2,1,0:T(8,128)}), f32[8,8,8,1152]{3,2,1,0:T(8,128)}, u32[]{:S(2)}, u32[]{:S(2)}) async-start(f32[8,8,8,1152]{3,2,1,0:T(8,128)} %bitcast.82), calls=%async_computation | async-start | bytes 4718592 | tf_op jit(solution)/shard_map/all_to_all | solution.py:309
  17.9 54.0 %collective-permute-start = (f32[512,1152]{1,0:T(8,128)}, f32[512,1152]{1,0:T(8,128)}, u32[]{:S(2)}, u32[]{:S(2)}) collective-permute-start(f32[512,1152]{1,0:T(8,128)} %copy-done.2), channel_id=1, source_target_pairs={{0,16},{8,24},{16,0},{24,8},{1,17},{9,25},{17,1},{25,9},{2,18},{10... | collective-permute-start | bytes 7077896 | tf_op jit(solution)/shard_map/ppermute | solution.py:301
  19.4 53.5 %collective-permute-start.1 = (f32[512,1152]{1,0:T(8,128)S(1)}, f32[512,1152]{1,0:T(8,128)}, u32[]{:S(2)}, u32[]{:S(2)}) collective-permute-start(f32[512,1152]{1,0:T(8,128)S(1)} %get-tuple-element.775.amps_ref), channel_id=1, source_target_pairs={{0,8},{8,0},{16,24},{24,16},{1,9},{9,1},{17,25},{25,17},{2,10},{10... | collective-permute-start | bytes 7077896 | tf_op jit(solution)/shard_map/ppermute | solution.py:301
  74.5 60.3 %all-to-all-start.1 = ((f32[8,8,8,1152]{3,2,1,0:T(8,128)}), f32[8,8,8,1152]{3,2,1,0:T(8,128)}, u32[]{:S(2)}, u32[]{:S(2)}) async-start(f32[8,8,8,1152]{3,2,1,0:T(8,128)} %bitcast.83), calls=%async_computation.1 | async-start | bytes 4718592 | tf_op jit(solution)/shard_map/all_to_all | solution.py:309
  79.2 124.0 %all-gather.8.cloned.1.call-start = ((), (), s32[]{:S(2)}) async-start(), calls=%async_computation.6 | async-start | bytes 4718592 | tf_op jit(solution)/shard_map/all_gather | solution.py:354
  79.7 54.0 %collective-permute-start.2 = (f32[512,1152]{1,0:T(8,128)}, f32[512,1152]{1,0:T(8,128)}, u32[]{:S(2)}, u32[]{:S(2)}) collective-permute-start(f32[512,1152]{1,0:T(8,128)} %copy-done.2), channel_id=1, source_target_pairs={{0,8},{8,0},{16,24},{24,16},{1,9},{9,1},{17,25},{25,17},{2,10},{10... | collective-permute-start | bytes 7077896 | tf_op jit(solution)/shard_map/ppermute | solution.py:301
  81.3 53.4 %collective-permute-start.3 = (f32[512,1152]{1,0:T(8,128)S(1)}, f32[512,1152]{1,0:T(8,128)}, u32[]{:S(2)}, u32[]{:S(2)}) collective-permute-start(f32[512,1152]{1,0:T(8,128)S(1)} %get-tuple-element.775.amps_ref), channel_id=1, source_target_pairs={{0,16},{8,24},{16,0},{24,8},{1,17},{9,25},{17,1},{25,9},{2,18},{10... | collective-permute-start | bytes 7077896 | tf_op jit(solution)/shard_map/ppermute | solution.py:301
  141.9 78.9 %collective-permute-start.4 = (f32[512,1152]{1,0:T(8,128)}, f32[512,1152]{1,0:T(8,128)}, u32[]{:S(2)}, u32[]{:S(2)}) collective-permute-start(f32[512,1152]{1,0:T(8,128)} %collective-permute-done.amps_ref), channel_id=1, source_target_pairs={{0,8},{8,0},{16,24},{24,16},{1,9},{9,1},{17,25},{25,17},{2,10},{10... | collective-permute-start | bytes 7077896 | tf_op jit(solution)/shard_map/ppermute | solution.py:301
  142.8 78.1 %collective-permute-start.5 = (f32[512,1152]{1,0:T(8,128)}, f32[512,1152]{1,0:T(8,128)}, u32[]{:S(2)}, u32[]{:S(2)}) collective-permute-start(f32[512,1152]{1,0:T(8,128)} %collective-permute-done.1.amps_ref), channel_id=1, source_target_pairs={{0,16},{8,24},{16,0},{24,8},{1,17},{9,25},{17,1},{25,9},{2,18},{10... | collective-permute-start | bytes 7077896 | tf_op jit(solution)/shard_map/ppermute | solution.py:301
  163.5 57.4 %collective-permute-start.6 = (f32[2,192,768]{2,1,0:T(8,128)}, f32[2,192,768]{2,1,0:T(8,128)}, u32[]{:S(2)}, u32[]{:S(2)}) collective-permute-start(f32[2,192,768]{2,1,0:T(8,128)} %get-tuple-element.808), channel_id=1, source_target_pairs={{0,16},{8,24},{16,0},{24,8},{1,17},{9,25},{17,1},{25,9},{2,18},{10... | collective-permute-start | bytes 3538952 | tf_op jit(solution)/shard_map/ppermute | solution.py:301
  164.5 56.3 %collective-permute-start.7 = (f32[2,192,768]{2,1,0:T(8,128)}, f32[2,192,768]{2,1,0:T(8,128)}, u32[]{:S(2)}, u32[]{:S(2)}) collective-permute-start(f32[2,192,768]{2,1,0:T(8,128)} %get-tuple-element.809), channel_id=1, source_target_pairs={{0,8},{8,0},{16,24},{24,16},{1,9},{9,1},{17,25},{25,17},{2,10},{10... | collective-permute-start | bytes 3538952 | tf_op jit(solution)/shard_map/ppermute | solution.py:301
  222.8 24.9 %collective-permute-start.8 = (f32[1,192,768]{2,1,0:T(8,128)}, f32[1,192,768]{2,1,0:T(8,128)S(1)}, u32[]{:S(2)}, u32[]{:S(2)}) collective-permute-start(f32[1,192,768]{2,1,0:T(8,128)} %slice_add_fusion.7), channel_id=1, source_target_pairs={{0,8},{8,0},{16,24},{24,16},{1,9},{9,1},{17,25},{25,17},{2,10},{10... | collective-permute-start | bytes 1769480 | tf_op jit(solution)/shard_map/ppermute | solution.py:301
  226.5 38.0 %collective-permute-start.10 = (f32[2,192,768]{2,1,0:T(8,128)}, f32[2,192,768]{2,1,0:T(8,128)}, u32[]{:S(2)}, u32[]{:S(2)}) collective-permute-start(f32[2,192,768]{2,1,0:T(8,128)} %get-tuple-element.832), channel_id=1, source_target_pairs={{0,16},{8,24},{16,0},{24,8},{1,17},{9,25},{17,1},{25,9},{2,18},{10... | collective-permute-start | bytes 3538952 | tf_op jit(solution)/shard_map/ppermute | solution.py:301
  227.8 36.7 %collective-permute-start.11 = (f32[2,192,768]{2,1,0:T(8,128)}, f32[2,192,768]{2,1,0:T(8,128)}, u32[]{:S(2)}, u32[]{:S(2)}) collective-permute-start(f32[2,192,768]{2,1,0:T(8,128)} %get-tuple-element.833), channel_id=1, source_target_pairs={{0,8},{8,0},{16,24},{24,16},{1,9},{9,1},{17,25},{25,17},{2,10},{10... | collective-permute-start | bytes 3538952 | tf_op jit(solution)/shard_map/ppermute | solution.py:301
  252.5 40.0 %all-to-all-start.5 = ((f32[8,48,768]{2,1,0:T(8,128)}), f32[8,48,768]{2,1,0:T(8,128)S(1)}, u32[]{:S(2)}, u32[]{:S(2)}) async-start(f32[8,48,768]{2,1,0:T(8,128)} %owner_blocks.4), calls=%async_computation.5 | async-start | bytes 2359296 | tf_op jit(solution)/shard_map/all_to_all | solution.py:390
  265.6 22.7 %collective-permute-start.12 = (f32[1,192,768]{2,1,0:T(8,128)S(1)}, f32[1,192,768]{2,1,0:T(8,128)S(1)}, u32[]{:S(2)}, u32[]{:S(2)}) collective-permute-start(f32[1,192,768]{2,1,0:T(8,128)S(1)} %slice_add_fusion.5), channel_id=1, source_target_pairs={{0,8},{8,0},{16,24},{24,16},{1,9},{9,1},{17,25},{25,17},{2,10},{10... | collective-permute-start | bytes 1769480 | tf_op jit(solution)/shard_map/ppermute | solution.py:301
  269.1 37.9 %collective-permute-start.14 = (f32[2,192,768]{2,1,0:T(8,128)}, f32[2,192,768]{2,1,0:T(8,128)}, u32[]{:S(2)}, u32[]{:S(2)}) collective-permute-start(f32[2,192,768]{2,1,0:T(8,128)} %get-tuple-element.854), channel_id=1, source_target_pairs={{0,16},{8,24},{16,0},{24,8},{1,17},{9,25},{17,1},{25,9},{2,18},{10... | collective-permute-start | bytes 3538952 | tf_op jit(solution)/shard_map/ppermute | solution.py:301
  270.3 36.8 %collective-permute-start.15 = (f32[2,192,768]{2,1,0:T(8,128)}, f32[2,192,768]{2,1,0:T(8,128)}, u32[]{:S(2)}, u32[]{:S(2)}) collective-permute-start(f32[2,192,768]{2,1,0:T(8,128)} %get-tuple-element.855), channel_id=1, source_target_pairs={{0,8},{8,0},{16,24},{24,16},{1,9},{9,1},{17,25},{25,17},{2,10},{10... | collective-permute-start | bytes 3538952 | tf_op jit(solution)/shard_map/ppermute | solution.py:301
  292.6 46.3 %all-to-all-start.4 = ((f32[8,48,768]{2,1,0:T(8,128)}), f32[8,48,768]{2,1,0:T(8,128)S(1)}, u32[]{:S(2)}, u32[]{:S(2)}) async-start(f32[8,48,768]{2,1,0:T(8,128)} %owner_blocks.5), calls=%async_computation.4 | async-start | bytes 2359296 | tf_op jit(solution)/shard_map/all_to_all | solution.py:390
  309.1 24.9 %collective-permute-start.16 = (f32[1,192,768]{2,1,0:T(8,128)}, f32[1,192,768]{2,1,0:T(8,128)S(1)}, u32[]{:S(2)}, u32[]{:S(2)}) collective-permute-start(f32[1,192,768]{2,1,0:T(8,128)} %slice_add_fusion.3), channel_id=1, source_target_pairs={{0,8},{8,0},{16,24},{24,16},{1,9},{9,1},{17,25},{25,17},{2,10},{10... | collective-permute-start | bytes 1769480 | tf_op jit(solution)/shard_map/ppermute | solution.py:301
  312.2 40.0 %collective-permute-start.18 = (f32[2,192,768]{2,1,0:T(8,128)}, f32[2,192,768]{2,1,0:T(8,128)}, u32[]{:S(2)}, u32[]{:S(2)}) collective-permute-start(f32[2,192,768]{2,1,0:T(8,128)} %get-tuple-element.870), channel_id=1, source_target_pairs={{0,16},{8,24},{16,0},{24,8},{1,17},{9,25},{17,1},{25,9},{2,18},{10... | collective-permute-start | bytes 3538952 | tf_op jit(solution)/shard_map/ppermute | solution.py:301
  313.4 38.8 %collective-permute-start.19 = (f32[2,192,768]{2,1,0:T(8,128)}, f32[2,192,768]{2,1,0:T(8,128)}, u32[]{:S(2)}, u32[]{:S(2)}) collective-permute-start(f32[2,192,768]{2,1,0:T(8,128)} %get-tuple-element.871), channel_id=1, source_target_pairs={{0,8},{8,0},{16,24},{24,16},{1,9},{9,1},{17,25},{25,17},{2,10},{10... | collective-permute-start | bytes 3538952 | tf_op jit(solution)/shard_map/ppermute | solution.py:301
  338.9 36.9 %all-to-all-start.3 = ((f32[8,48,768]{2,1,0:T(8,128)}), f32[8,48,768]{2,1,0:T(8,128)S(1)}, u32[]{:S(2)}, u32[]{:S(2)}) async-start(f32[8,48,768]{2,1,0:T(8,128)} %owner_blocks.6), calls=%async_computation.3 | async-start | bytes 2359296 | tf_op jit(solution)/shard_map/all_to_all | solution.py:390
  375.8 34.0 %all-to-all-start.2 = ((f32[8,48,768]{2,1,0:T(8,128)}), f32[8,48,768]{2,1,0:T(8,128)S(1)}, u32[]{:S(2)}, u32[]{:S(2)}) async-start(f32[8,48,768]{2,1,0:T(8,128)} %owner_blocks.7), calls=%async_computation.2 | async-start | bytes 2359296 | tf_op jit(solution)/shard_map/all_to_all | solution.py:390
  (37 other events, 685.0 us)
Sparse Core Ops, SparseCore 0:
  142.0 46.6 all-gather.7

commit v3 on v2

--- a/solution.py
+++ b/solution.py
@@ -54,7 +54,7 @@
         out_specs=[pl.BlockSpec((height, depth * occ), lambda c: (c, 0))] * 2,
         out_shape=[shape, shape],
         scratch_shapes=[
-            pltpu.VMEM((height * 8, 128), jnp.float32),
+            pltpu.VMEM((height * 8 + 8, 128), jnp.float32),
             pltpu.VMEM((height, depth * occ), jnp.float32),
         ],
         compiler_params=PARAMS,
@@ -195,7 +195,7 @@
             ],
             out_specs=block,
             scratch_shapes=[
-                pltpu.VMEM((height * pad, 128), jnp.float32),
+                pltpu.VMEM((height * pad + pad, 128), jnp.float32),
                 pltpu.VMEM((height, columns), jnp.float32),
             ],
         ),

time: 427 us -> 427 us (level)
  no operation moved by 1% of the time
where the time goes in v3:
time: 427 us; the launch traced here: 422 us
  Pallas kernels  192 us (45%)
  waiting for transfers between devices  119 us (28%)
  starting transfers between devices  54 us (13%)
  local copies, waits for them, and re-layouts  20.4 us (5%)
  other arithmetic  19 us (4%)
  between operations  16.5 us (4%)
    ppermute x22, waiting for transfers between devices, swap(): return lax.ppermute(value, 'row', [(i, i ^ flip) for i in range(row_count)])  113 us
    pallas_call x8, Pallas kernels, ladder_term(): pl.pallas_call(functools.partial(ladder_kernel, fresh), grid_spec=pltpu.P...  77.5 us
    pallas_call x4, Pallas kernels, cycle_sums(): pl.pallas_call(cycle_kernel, grid_spec=pltpu.PrefetchScalarGridSpec(num_s...  70.2 us
    ppermute x22, starting transfers between devices, swap(): return lax.ppermute(value, 'row', [(i, i ^ flip) for i in range(row_count)])  23.6 us
    all_to_all x4, starting transfers between devices, to_owner(): lax.all_to_all(blocks, 'col', split_axis=0, concat_axis=0, tiled=True)  18.6 us
    pallas_call x4, Pallas kernels, with_cycle(): pl.pallas_call(functools.partial(update_kernel, occ, occ_local), grid_spe...  16.5 us
    pallas_call x2, Pallas kernels, to_cycle_rows(): pl.pallas_call(functools.partial(to_cycle_kernel, occ), grid=(count,), in...  14.6 us
    pallas_call x4, Pallas kernels, owner_blocks(): pl.pallas_call(functools.partial(owner_kernel, occ_local), grid=(1,), in_...  12.7 us
  transfers between devices with their start and end apart: 29, of which 10 were waited for; matrix products, arithmetic and copies ran while one was open for 6% of the time, Pallas kernels for 43%

profile of v3, /device:TPU:0, one launch (start us, length us, event | category | flops | bytes accessed | tf_op | source)
XLA Modules:
  0.0 421.9 jit_solution(15701739704361133452)
XLA Ops:
  11.4 6.5 %all-to-all-start = ((f32[8,8,8,1152]{3,2,1,0:T(8,128)}), f32[8,8,8,1152]{3,2,1,0:T(8,128)}, u32[]{:S(2)}, u32[]{:S(2)}) async-start(f32[8,8,8,1152]{3,2,1,0:T(8,128)} %bitcast.82), calls=%async_computation | async-start | bytes 4718592 | tf_op jit(solution)/shard_map/all_to_all | solution.py:309
  29.4 42.5 %collective-permute-done.amps_ref = f32[512,1152]{1,0:T(8,128)} collective-permute-done((f32[512,1152]{1,0:T(8,128)}, f32[512,1152]{1,0:T(8,128)}, u32[]{:S(2)}, u32[]{:S(2)}) %collective-permute-start) | collective-permute-done | bytes 2359328 | tf_op jit(solution)/shard_map/ppermute | solution.py:301
  74.5 4.7 %all-to-all-start.1 = ((f32[8,8,8,1152]{3,2,1,0:T(8,128)}), f32[8,8,8,1152]{3,2,1,0:T(8,128)}, u32[]{:S(2)}, u32[]{:S(2)}) async-start(f32[8,8,8,1152]{3,2,1,0:T(8,128)} %bitcast.83), calls=%async_computation.1 | async-start | bytes 4718592 | tf_op jit(solution)/shard_map/all_to_all | solution.py:309
  84.2 7.4 %to_cycle_rows.2 = (bf16[768,768]{1,0:T(8,128)(2,1)}, bf16[768,768]{1,0:T(8,128)(2,1)}) custom-call(f32[8,8,8,1152]{3,2,1,0:T(8,128)} %all-to-all-done.moved_ref), custom_call_target="tpu_custom_call" | custom-call | tf_op jit(solution)/shard_map/to_cycle_rows/pallas_call | solution.py:50
  93.3 40.4 %collective-permute-done.2.amps_ref = f32[512,1152]{1,0:T(8,128)} collective-permute-done((f32[512,1152]{1,0:T(8,128)}, f32[512,1152]{1,0:T(8,128)}, u32[]{:S(2)}, u32[]{:S(2)}) %collective-permute-start.2) | collective-permute-done | bytes 2359328 | tf_op jit(solution)/shard_map/ppermute | solution.py:301
  134.7 7.2 %to_cycle_rows.3 = (bf16[768,768]{1,0:T(8,128)(2,1)}, bf16[768,768]{1,0:T(8,128)(2,1)}) custom-call(f32[8,8,8,1152]{3,2,1,0:T(8,128)} %all-to-all-done.1.moved_ref), custom_call_target="tpu_custom_call" | custom-call | tf_op jit(solution)/shard_map/to_cycle_rows/pallas_call | solution.py:50
  145.8 17.7 %cycle_sums.4 = (f32[2,192,768]{2,1,0:T(8,128)}, f32[2,192,768]{2,1,0:T(8,128)}, f32[2,192,768]{2,1,0:T(8,128)}, f32[2,192,768]{2,1,0:T(8,128)}) custom-call(s32[1]{0:T(128)} %bitcast.8.base, f32[6144,1536]{1,0:T(8,128)} %ints_ref.7, s32[6144,1]{1,0:T(8,128)} %copy.70.rows_ref, s32[1,1536]{1,0:T(1,128)} %broadcast_in_dim.12.own_ref, ...), custom_call_target="tpu_custom_call" | custom-call | tf_op jit(solution)/shard_map/cycle_sums/pallas_call | solution.py:109
  168.1 17.5 %cycle_sums.5 = (f32[2,192,768]{2,1,0:T(8,128)}, f32[2,192,768]{2,1,0:T(8,128)}, f32[2,192,768]{2,1,0:T(8,128)}, f32[2,192,768]{2,1,0:T(8,128)}) custom-call(s32[1]{0:T(128)} %bitcast.8.base, f32[6144,1536]{1,0:T(8,128)} %ints_ref.7, s32[6144,1]{1,0:T(8,128)} %copy.70.rows_ref, s32[1,1536]{1,0:T(1,128)} %broadcast_in_dim.12.own_ref, ...), custom_call_target="tpu_custom_call" | custom-call | tf_op jit(solution)/shard_map/cycle_sums/pallas_call | solution.py:109
  185.7 17.5 %cycle_sums.6 = (f32[2,192,768]{2,1,0:T(8,128)}, f32[2,192,768]{2,1,0:T(8,128)}, f32[2,192,768]{2,1,0:T(8,128)}, f32[2,192,768]{2,1,0:T(8,128)}) custom-call(s32[1]{0:T(128)} %bitcast.8.base, f32[6144,1536]{1,0:T(8,128)} %ints_ref.7, s32[6144,1]{1,0:T(8,128)} %copy.70.rows_ref, s32[1,1536]{1,0:T(1,128)} %broadcast_in_dim.12.own_ref, ...), custom_call_target="tpu_custom_call" | custom-call | tf_op jit(solution)/shard_map/cycle_sums/pallas_call | solution.py:109
  203.2 9.4 %ladder_term.20.refs_0_ = f32[1024,1152]{1,0:T(8,128)} custom-call(s32[1]{0:T(128)} %bitcast.12.start, f32[8,1024,128]{2,1,0:T(8,128)} %bitcast.72, s32[8,1,512]{2,1,0:T(1,128)} %broadcast_in_dim.13.rank_ref, s32[8,1,512]{2,1,0:T(1,128)} %broadcast_xor_fusion.3.label_ref, s32[1024,1]{1,0:T(8,128)} %copy.77.own_ref, f32[512,1152]{1,0:T(8,128)} %copy-done.2), custom_call_target="tpu_custom_call" | custom-call | tf_op jit(solution)/shard_map/ladder_term/pallas_call | solution.py:249
  212.6 8.3 %collective-permute-done.6.refs_1_ = f32[2,192,768]{2,1,0:T(8,128)} collective-permute-done((f32[2,192,768]{2,1,0:T(8,128)}, f32[2,192,768]{2,1,0:T(8,128)}, u32[]{:S(2)}, u32[]{:S(2)}) %collective-permute-start.6) | collective-permute-done | bytes 1179680 | tf_op jit(solution)/shard_map/ppermute | solution.py:301
  228.9 9.0 %ladder_term.21.refs_0_ = f32[1024,1152]{1,0:T(8,128)} custom-call(s32[1]{0:T(128)} %bitcast.14.start, f32[8,1024,128]{2,1,0:T(8,128)} %bitcast.73, s32[8,1,512]{2,1,0:T(1,128)} %broadcast_in_dim.13.rank_ref, s32[8,1,512]{2,1,0:T(1,128)} %broadcast_xor_fusion.3.label_ref, s32[1024,1]{1,0:T(8,128)} %copy.77.own_ref, ...), custom_call_target="tpu_custom_call", output_to_operand_aliasing={{}: (6, {})} | custom-call | tf_op jit(solution)/shard_map/ladder_term/pallas_call | solution.py:249
  237.9 9.8 %ladder_term.22.refs_0_ = f32[1024,1152]{1,0:T(8,128)} custom-call(s32[1]{0:T(128)} %bitcast.13.start, f32[8,1024,128]{2,1,0:T(8,128)} %bitcast.74, s32[8,1,512]{2,1,0:T(1,128)} %broadcast_in_dim.13.rank_ref, s32[8,1,512]{2,1,0:T(1,128)} %broadcast_xor_fusion.3.label_ref, s32[1024,1]{1,0:T(8,128)} %copy.77.own_ref, ...), custom_call_target="tpu_custom_call", output_to_operand_aliasing={{}: (6, {})} | custom-call | tf_op jit(solution)/shard_map/ladder_term/pallas_call | solution.py:249
  256.8 7.7 %collective-permute-done.10.refs_1_ = f32[2,192,768]{2,1,0:T(8,128)} collective-permute-done((f32[2,192,768]{2,1,0:T(8,128)}, f32[2,192,768]{2,1,0:T(8,128)}, u32[]{:S(2)}, u32[]{:S(2)}) %collective-permute-start.10) | collective-permute-done | bytes 1179680 | tf_op jit(solution)/shard_map/ppermute | solution.py:301
  271.0 17.4 %cycle_sums.7 = (f32[2,192,768]{2,1,0:T(8,128)}, f32[2,192,768]{2,1,0:T(8,128)}, f32[2,192,768]{2,1,0:T(8,128)}, f32[2,192,768]{2,1,0:T(8,128)}) custom-call(s32[1]{0:T(128)} %bitcast.8.base, f32[6144,1536]{1,0:T(8,128)} %ints_ref.7, s32[6144,1]{1,0:T(8,128)} %copy.70.rows_ref, s32[1,1536]{1,0:T(1,128)} %broadcast_in_dim.12.own_ref, ...), custom_call_target="tpu_custom_call" | custom-call | tf_op jit(solution)/shard_map/cycle_sums/pallas_call | solution.py:109
  297.1 9.9 %ladder_term.23.refs_0_ = f32[1024,1152]{1,0:T(8,128)} custom-call(s32[1]{0:T(128)} %bitcast.11.start, f32[8,1024,128]{2,1,0:T(8,128)} %bitcast.75, s32[8,1,512]{2,1,0:T(1,128)} %broadcast_in_dim.13.rank_ref, s32[8,1,512]{2,1,0:T(1,128)} %broadcast_xor_fusion.3.label_ref, s32[1024,1]{1,0:T(8,128)} %copy.77.own_ref, ...), custom_call_target="tpu_custom_call", output_to_operand_aliasing={{}: (6, {})} | custom-call | tf_op jit(solution)/shard_map/ladder_term/pallas_call | solution.py:249
  314.3 9.8 %ladder_term.24.refs_0_ = f32[1024,1152]{1,0:T(8,128)} custom-call(s32[1]{0:T(128)} %bitcast.10.start, f32[8,1024,128]{2,1,0:T(8,128)} %bitcast.76, s32[8,1,512]{2,1,0:T(1,128)} %broadcast_in_dim.13.rank_ref, s32[8,1,512]{2,1,0:T(1,128)} %broadcast_xor_fusion.3.label_ref, s32[1024,1]{1,0:T(8,128)} %copy.77.own_ref, ...), custom_call_target="tpu_custom_call", output_to_operand_aliasing={{}: (6, {})} | custom-call | tf_op jit(solution)/shard_map/ladder_term/pallas_call | solution.py:249
  324.2 9.8 %ladder_term.25.refs_0_ = f32[1024,1152]{1,0:T(8,128)} custom-call(s32[1]{0:T(128)} %bitcast.start, f32[8,1024,128]{2,1,0:T(8,128)} %bitcast.77, s32[8,1,512]{2,1,0:T(1,128)} %broadcast_in_dim.13.rank_ref, s32[8,1,512]{2,1,0:T(1,128)} %broadcast_xor_fusion.3.label_ref, s32[1024,1]{1,0:T(8,128)} %copy.77.own_ref, ...), custom_call_target="tpu_custom_call", output_to_operand_aliasing={{}: (6, {})} | custom-call | tf_op jit(solution)/shard_map/ladder_term/pallas_call | solution.py:249
  338.9 5.2 %all-to-all-start.3 = ((f32[8,48,768]{2,1,0:T(8,128)}), f32[8,48,768]{2,1,0:T(8,128)S(1)}, u32[]{:S(2)}, u32[]{:S(2)}) async-start(f32[8,48,768]{2,1,0:T(8,128)} %owner_blocks.6), calls=%async_computation.3 | async-start | bytes 2359296 | tf_op jit(solution)/shard_map/all_to_all | solution.py:390
  344.1 8.1 %collective-permute-done.18.refs_1_ = f32[2,192,768]{2,1,0:T(8,128)} collective-permute-done((f32[2,192,768]{2,1,0:T(8,128)}, f32[2,192,768]{2,1,0:T(8,128)}, u32[]{:S(2)}, u32[]{:S(2)}) %collective-permute-start.18) | collective-permute-done | bytes 1179680 | tf_op jit(solution)/shard_map/ppermute | solution.py:301
  358.0 9.8 %ladder_term.26.refs_0_ = f32[1024,1152]{1,0:T(8,128)} custom-call(s32[1]{0:T(128)} %bitcast.15.start, f32[8,1024,128]{2,1,0:T(8,128)} %bitcast.78, s32[8,1,512]{2,1,0:T(1,128)} %broadcast_in_dim.13.rank_ref, s32[8,1,512]{2,1,0:T(1,128)} %broadcast_xor_fusion.3.label_ref, s32[1024,1]{1,0:T(8,128)} %copy.77.own_ref, ...), custom_call_target="tpu_custom_call", output_to_operand_aliasing={{}: (6, {})} | custom-call | tf_op jit(solution)/shard_map/ladder_term/pallas_call | solution.py:249
  375.8 4.6 %all-to-all-start.2 = ((f32[8,48,768]{2,1,0:T(8,128)}), f32[8,48,768]{2,1,0:T(8,128)S(1)}, u32[]{:S(2)}, u32[]{:S(2)}) async-start(f32[8,48,768]{2,1,0:T(8,128)} %owner_blocks.7), calls=%async_computation.2 | async-start | bytes 2359296 | tf_op jit(solution)/shard_map/all_to_all | solution.py:390
  381.4 9.9 %ladder_term.27.ladder_ref = f32[1024,1152]{1,0:T(8,128)} custom-call(s32[1]{0:T(128)} %bitcast.16.start, f32[8,1024,128]{2,1,0:T(8,128)} %bitcast.79, s32[8,1,512]{2,1,0:T(1,128)} %broadcast_in_dim.13.rank_ref, s32[8,1,512]{2,1,0:T(1,128)} %broadcast_xor_fusion.3.label_ref, s32[1024,1]{1,0:T(8,128)} %copy.77.own_ref, ...), custom_call_target="tpu_custom_call", output_to_operand_aliasing={{}: (6, {})} | custom-call | tf_op jit(solution)/shard_map/ladder_term/pallas_call | solution.py:249
  403.7 6.0 %all-to-all-done.2.back_ref = f32[8,48,768]{2,1,0:T(8,128)S(1)} async-done(((f32[8,48,768]{2,1,0:T(8,128)}), f32[8,48,768]{2,1,0:T(8,128)S(1)}, u32[]{:S(2)}, u32[]{:S(2)}) %all-to-all-start.2) | async-done | bytes 1179680 | tf_op jit(solution)/shard_map/all_to_all | solution.py:390
  (166 shorter events, 109.1 us)
Async XLA Ops:
  11.4 61.5 %all-to-all-start = ((f32[8,8,8,1152]{3,2,1,0:T(8,128)}), f32[8,8,8,1152]{3,2,1,0:T(8,128)}, u32[]{:S(2)}, u32[]{:S(2)}) async-start(f32[8,8,8,1152]{3,2,1,0:T(8,128)} %bitcast.82), calls=%async_computation | async-start | bytes 4718592 | tf_op jit(solution)/shard_map/all_to_all | solution.py:309
  17.9 54.0 %collective-permute-start = (f32[512,1152]{1,0:T(8,128)}, f32[512,1152]{1,0:T(8,128)}, u32[]{:S(2)}, u32[]{:S(2)}) collective-permute-start(f32[512,1152]{1,0:T(8,128)} %copy-done.2), channel_id=1, source_target_pairs={{0,16},{8,24},{16,0},{24,8},{1,17},{9,25},{17,1},{25,9},{2,18},{10... | collective-permute-start | bytes 7077896 | tf_op jit(solution)/shard_map/ppermute | solution.py:301
  19.4 53.5 %collective-permute-start.1 = (f32[512,1152]{1,0:T(8,128)S(1)}, f32[512,1152]{1,0:T(8,128)}, u32[]{:S(2)}, u32[]{:S(2)}) collective-permute-start(f32[512,1152]{1,0:T(8,128)S(1)} %get-tuple-element.775.amps_ref), channel_id=1, source_target_pairs={{0,8},{8,0},{16,24},{24,16},{1,9},{9,1},{17,25},{25,17},{2,10},{10... | collective-permute-start | bytes 7077896 | tf_op jit(solution)/shard_map/ppermute | solution.py:301
  74.5 60.3 %all-to-all-start.1 = ((f32[8,8,8,1152]{3,2,1,0:T(8,128)}), f32[8,8,8,1152]{3,2,1,0:T(8,128)}, u32[]{:S(2)}, u32[]{:S(2)}) async-start(f32[8,8,8,1152]{3,2,1,0:T(8,128)} %bitcast.83), calls=%async_computation.1 | async-start | bytes 4718592 | tf_op jit(solution)/shard_map/all_to_all | solution.py:309
  79.2 124.0 %all-gather.8.cloned.1.call-start = ((), (), s32[]{:S(2)}) async-start(), calls=%async_computation.6 | async-start | bytes 4718592 | tf_op jit(solution)/shard_map/all_gather | solution.py:354
  79.7 54.0 %collective-permute-start.2 = (f32[512,1152]{1,0:T(8,128)}, f32[512,1152]{1,0:T(8,128)}, u32[]{:S(2)}, u32[]{:S(2)}) collective-permute-start(f32[512,1152]{1,0:T(8,128)} %copy-done.2), channel_id=1, source_target_pairs={{0,8},{8,0},{16,24},{24,16},{1,9},{9,1},{17,25},{25,17},{2,10},{10... | collective-permute-start | bytes 7077896 | tf_op jit(solution)/shard_map/ppermute | solution.py:301
  81.3 53.4 %collective-permute-start.3 = (f32[512,1152]{1,0:T(8,128)S(1)}, f32[512,1152]{1,0:T(8,128)}, u32[]{:S(2)}, u32[]{:S(2)}) collective-permute-start(f32[512,1152]{1,0:T(8,128)S(1)} %get-tuple-element.775.amps_ref), channel_id=1, source_target_pairs={{0,16},{8,24},{16,0},{24,8},{1,17},{9,25},{17,1},{25,9},{2,18},{10... | collective-permute-start | bytes 7077896 | tf_op jit(solution)/shard_map/ppermute | solution.py:301
  141.9 78.9 %collective-permute-start.4 = (f32[512,1152]{1,0:T(8,128)}, f32[512,1152]{1,0:T(8,128)}, u32[]{:S(2)}, u32[]{:S(2)}) collective-permute-start(f32[512,1152]{1,0:T(8,128)} %collective-permute-done.amps_ref), channel_id=1, source_target_pairs={{0,8},{8,0},{16,24},{24,16},{1,9},{9,1},{17,25},{25,17},{2,10},{10... | collective-permute-start | bytes 7077896 | tf_op jit(solution)/shard_map/ppermute | solution.py:301
  142.8 78.1 %collective-permute-start.5 = (f32[512,1152]{1,0:T(8,128)}, f32[512,1152]{1,0:T(8,128)}, u32[]{:S(2)}, u32[]{:S(2)}) collective-permute-start(f32[512,1152]{1,0:T(8,128)} %collective-permute-done.1.amps_ref), channel_id=1, source_target_pairs={{0,16},{8,24},{16,0},{24,8},{1,17},{9,25},{17,1},{25,9},{2,18},{10... | collective-permute-start | bytes 7077896 | tf_op jit(solution)/shard_map/ppermute | solution.py:301
  163.5 57.4 %collective-permute-start.6 = (f32[2,192,768]{2,1,0:T(8,128)}, f32[2,192,768]{2,1,0:T(8,128)}, u32[]{:S(2)}, u32[]{:S(2)}) collective-permute-start(f32[2,192,768]{2,1,0:T(8,128)} %get-tuple-element.808), channel_id=1, source_target_pairs={{0,16},{8,24},{16,0},{24,8},{1,17},{9,25},{17,1},{25,9},{2,18},{10... | collective-permute-start | bytes 3538952 | tf_op jit(solution)/shard_map/ppermute | solution.py:301
  164.5 56.3 %collective-permute-start.7 = (f32[2,192,768]{2,1,0:T(8,128)}, f32[2,192,768]{2,1,0:T(8,128)}, u32[]{:S(2)}, u32[]{:S(2)}) collective-permute-start(f32[2,192,768]{2,1,0:T(8,128)} %get-tuple-element.809), channel_id=1, source_target_pairs={{0,8},{8,0},{16,24},{24,16},{1,9},{9,1},{17,25},{25,17},{2,10},{10... | collective-permute-start | bytes 3538952 | tf_op jit(solution)/shard_map/ppermute | solution.py:301
  222.8 24.9 %collective-permute-start.8 = (f32[1,192,768]{2,1,0:T(8,128)}, f32[1,192,768]{2,1,0:T(8,128)S(1)}, u32[]{:S(2)}, u32[]{:S(2)}) collective-permute-start(f32[1,192,768]{2,1,0:T(8,128)} %slice_add_fusion.7), channel_id=1, source_target_pairs={{0,8},{8,0},{16,24},{24,16},{1,9},{9,1},{17,25},{25,17},{2,10},{10... | collective-permute-start | bytes 1769480 | tf_op jit(solution)/shard_map/ppermute | solution.py:301
  226.5 38.0 %collective-permute-start.10 = (f32[2,192,768]{2,1,0:T(8,128)}, f32[2,192,768]{2,1,0:T(8,128)}, u32[]{:S(2)}, u32[]{:S(2)}) collective-permute-start(f32[2,192,768]{2,1,0:T(8,128)} %get-tuple-element.832), channel_id=1, source_target_pairs={{0,16},{8,24},{16,0},{24,8},{1,17},{9,25},{17,1},{25,9},{2,18},{10... | collective-permute-start | bytes 3538952 | tf_op jit(solution)/shard_map/ppermute | solution.py:301
  227.8 36.7 %collective-permute-start.11 = (f32[2,192,768]{2,1,0:T(8,128)}, f32[2,192,768]{2,1,0:T(8,128)}, u32[]{:S(2)}, u32[]{:S(2)}) collective-permute-start(f32[2,192,768]{2,1,0:T(8,128)} %get-tuple-element.833), channel_id=1, source_target_pairs={{0,8},{8,0},{16,24},{24,16},{1,9},{9,1},{17,25},{25,17},{2,10},{10... | collective-permute-start | bytes 3538952 | tf_op jit(solution)/shard_map/ppermute | solution.py:301
  252.5 40.1 %all-to-all-start.5 = ((f32[8,48,768]{2,1,0:T(8,128)}), f32[8,48,768]{2,1,0:T(8,128)S(1)}, u32[]{:S(2)}, u32[]{:S(2)}) async-start(f32[8,48,768]{2,1,0:T(8,128)} %owner_blocks.4), calls=%async_computation.5 | async-start | bytes 2359296 | tf_op jit(solution)/shard_map/all_to_all | solution.py:390
  265.6 22.7 %collective-permute-start.12 = (f32[1,192,768]{2,1,0:T(8,128)S(1)}, f32[1,192,768]{2,1,0:T(8,128)S(1)}, u32[]{:S(2)}, u32[]{:S(2)}) collective-permute-start(f32[1,192,768]{2,1,0:T(8,128)S(1)} %slice_add_fusion.5), channel_id=1, source_target_pairs={{0,8},{8,0},{16,24},{24,16},{1,9},{9,1},{17,25},{25,17},{2,10},{10... | collective-permute-start | bytes 1769480 | tf_op jit(solution)/shard_map/ppermute | solution.py:301
  269.1 37.9 %collective-permute-start.14 = (f32[2,192,768]{2,1,0:T(8,128)}, f32[2,192,768]{2,1,0:T(8,128)}, u32[]{:S(2)}, u32[]{:S(2)}) collective-permute-start(f32[2,192,768]{2,1,0:T(8,128)} %get-tuple-element.854), channel_id=1, source_target_pairs={{0,16},{8,24},{16,0},{24,8},{1,17},{9,25},{17,1},{25,9},{2,18},{10... | collective-permute-start | bytes 3538952 | tf_op jit(solution)/shard_map/ppermute | solution.py:301
  270.3 36.8 %collective-permute-start.15 = (f32[2,192,768]{2,1,0:T(8,128)}, f32[2,192,768]{2,1,0:T(8,128)}, u32[]{:S(2)}, u32[]{:S(2)}) collective-permute-start(f32[2,192,768]{2,1,0:T(8,128)} %get-tuple-element.855), channel_id=1, source_target_pairs={{0,8},{8,0},{16,24},{24,16},{1,9},{9,1},{17,25},{25,17},{2,10},{10... | collective-permute-start | bytes 3538952 | tf_op jit(solution)/shard_map/ppermute | solution.py:301
  292.6 46.3 %all-to-all-start.4 = ((f32[8,48,768]{2,1,0:T(8,128)}), f32[8,48,768]{2,1,0:T(8,128)S(1)}, u32[]{:S(2)}, u32[]{:S(2)}) async-start(f32[8,48,768]{2,1,0:T(8,128)} %owner_blocks.5), calls=%async_computation.4 | async-start | bytes 2359296 | tf_op jit(solution)/shard_map/all_to_all | solution.py:390
  309.1 24.9 %collective-permute-start.16 = (f32[1,192,768]{2,1,0:T(8,128)}, f32[1,192,768]{2,1,0:T(8,128)S(1)}, u32[]{:S(2)}, u32[]{:S(2)}) collective-permute-start(f32[1,192,768]{2,1,0:T(8,128)} %slice_add_fusion.3), channel_id=1, source_target_pairs={{0,8},{8,0},{16,24},{24,16},{1,9},{9,1},{17,25},{25,17},{2,10},{10... | collective-permute-start | bytes 1769480 | tf_op jit(solution)/shard_map/ppermute | solution.py:301
  312.2 40.0 %collective-permute-start.18 = (f32[2,192,768]{2,1,0:T(8,128)}, f32[2,192,768]{2,1,0:T(8,128)}, u32[]{:S(2)}, u32[]{:S(2)}) collective-permute-start(f32[2,192,768]{2,1,0:T(8,128)} %get-tuple-element.870), channel_id=1, source_target_pairs={{0,16},{8,24},{16,0},{24,8},{1,17},{9,25},{17,1},{25,9},{2,18},{10... | collective-permute-start | bytes 3538952 | tf_op jit(solution)/shard_map/ppermute | solution.py:301
  313.4 38.8 %collective-permute-start.19 = (f32[2,192,768]{2,1,0:T(8,128)}, f32[2,192,768]{2,1,0:T(8,128)}, u32[]{:S(2)}, u32[]{:S(2)}) collective-permute-start(f32[2,192,768]{2,1,0:T(8,128)} %get-tuple-element.871), channel_id=1, source_target_pairs={{0,8},{8,0},{16,24},{24,16},{1,9},{9,1},{17,25},{25,17},{2,10},{10... | collective-permute-start | bytes 3538952 | tf_op jit(solution)/shard_map/ppermute | solution.py:301
  338.9 36.9 %all-to-all-start.3 = ((f32[8,48,768]{2,1,0:T(8,128)}), f32[8,48,768]{2,1,0:T(8,128)S(1)}, u32[]{:S(2)}, u32[]{:S(2)}) async-start(f32[8,48,768]{2,1,0:T(8,128)} %owner_blocks.6), calls=%async_computation.3 | async-start | bytes 2359296 | tf_op jit(solution)/shard_map/all_to_all | solution.py:390
  375.8 34.0 %all-to-all-start.2 = ((f32[8,48,768]{2,1,0:T(8,128)}), f32[8,48,768]{2,1,0:T(8,128)S(1)}, u32[]{:S(2)}, u32[]{:S(2)}) async-start(f32[8,48,768]{2,1,0:T(8,128)} %owner_blocks.7), calls=%async_computation.2 | async-start | bytes 2359296 | tf_op jit(solution)/shard_map/all_to_all | solution.py:390
  (37 other events, 685.0 us)
Sparse Core Ops, SparseCore 0:
  142.0 46.6 all-gather.7
